TPU v7x, 32 devices: a whole 2x2x4 slice. The times are simulated.
32 devices in a mesh: groups: 2 (over y), seq: 4 (over z), weight: 4 (over x, core).
Axes of the slice: x: 2, y: 2, z: 4, core: 2. Of those that a mesh axis runs over, the one named last changes fastest.
Arguments:
- tokens: bfloat16 [8, 512, 1536], P(('groups', 'weight'), 'seq'), parts along dimension 0, may hold values from -20 to 20
- upstream_grad: bfloat16 [8, 512, 1536], P(('groups', 'weight'), 'seq'), parts along dimension 0, may hold values from -6 to 6
- norm_gain: float32 [1536], replicated, may hold values from 0.5 to 1.5
- norm_bias: float32 [1536], replicated, may hold values from -3 to 3
- input_codes: bfloat16 [1536, 2304], P('weight'), may hold values from -10 to 10
- input_scales: float32 [12, 18], P('weight'), may hold values from 0.02 to 0.06
- input_bias: float32 [2304], replicated, may hold values from -3 to 3
- output_codes: bfloat16 [768, 1536], replicated, may hold values from -4 to 4
- output_scales: float32 [6, 12], replicated, may hold values from 0.02 to 0.06
- layer_scale: float32 [1536], replicated, may hold values from 0.3 to 3
Outputs:
- input_grad: float32 [8, 512, 1536], P(('groups', 'weight'), 'seq'), parts along dimension 0
There are 2 independent parts, one for each index of `groups`. A program takes and returns all parts, laid end to end along the dimension named above; an argument that names none is the same for every part. Nothing has to cross between parts.
All inputs are finite; a program needn't handle non-finite values.
Results may differ from a plain program's by a relative error of at most 0.024.
Values may be sent and summed in bfloat16 or wider, within the bound.
A program may use at most 128 MiB of HBM per device.

v0:
```python
import functools
import math

import jax
import jax.numpy as jnp
from jax import lax
from jax.experimental import pallas as pl
from jax.experimental.pallas import tpu as pltpu
from jax.sharding import PartitionSpec as P

HEADS = 12
HEAD_DIM = 64
QBLOCK = 128
HD = 768


def dequantize(codes, scales):
    expanded = jnp.repeat(jnp.repeat(scales, QBLOCK, axis=0), QBLOCK, axis=1)
    return (codes.astype(jnp.float32) * expanded).astype(jnp.bfloat16)


def normalize(rows, gain, shift):
    mean_value = jnp.mean(rows, axis=-1, keepdims=True)
    centered = rows - mean_value
    variance = jnp.mean(centered * centered, axis=-1, keepdims=True)
    inverse = lax.rsqrt(variance + 1e-06)
    normed = centered * inverse
    return (normed, inverse, (normed * gain + shift).astype(jnp.bfloat16))


def norm_backward(grad_norm, normed, inverse, gain):
    grad_hat = grad_norm * gain
    first_mean = jnp.mean(grad_hat, axis=-1, keepdims=True)
    second_mean = jnp.mean(grad_hat * normed, axis=-1, keepdims=True)
    return inverse * (grad_hat - first_mean - normed * second_mean)


def score_block(queries, head_grads, pair_block):
    row_count = pair_block.shape[0]
    keys_blk = pair_block[:, :HD].reshape(row_count, HEADS, HEAD_DIM)
    values_blk = pair_block[:, HD:].reshape(row_count, HEADS, HEAD_DIM)
    scores = jnp.einsum(
        "qhd,khd->hqk", queries, keys_blk, preferred_element_type=jnp.float32
    ) * HEAD_DIM ** (-0.5)
    dprob = jnp.einsum("qhd,khd->hqk", head_grads, values_blk, preferred_element_type=jnp.float32)
    return (keys_blk, scores, dprob)


def update_stats(statistics, queries, head_grads, pair_rows):
    sub_size = math.gcd(pair_rows.shape[0], 512)

    def visit_block(block_index, running):
        run_max, run_total, run_mix = running
        pair_block = lax.dynamic_slice_in_dim(pair_rows, block_index * sub_size, sub_size, 0)
        keys_blk, scores, dprob = score_block(queries, head_grads, pair_block)
        new_max = jnp.maximum(run_max, jnp.max(scores, axis=-1))
        factor = jnp.exp(run_max - new_max)
        expo = jnp.exp(scores - new_max[..., None])
        return (
            new_max,
            run_total * factor + jnp.sum(expo, axis=-1),
            run_mix * factor + jnp.sum(expo * dprob, axis=-1),
        )

    return lax.fori_loop(0, pair_rows.shape[0] // sub_size, visit_block, statistics)


def block_backward(queries, head_grads, pair_block, log_total, row_delta):
    keys_blk, scores, dprob = score_block(queries, head_grads, pair_block)
    weights = jnp.exp(scores - log_total[..., None])
    prob_weights = weights.astype(jnp.bfloat16)
    dscore = (weights * (dprob - row_delta[..., None])).astype(jnp.bfloat16)
    return (keys_blk, prob_weights, dscore)


def key_terms_from(queries, head_grads, prob_weights, dscore):
    key_part = jnp.einsum(
        "hqk,qhd->khd", dscore, queries, preferred_element_type=jnp.float32
    ) * HEAD_DIM ** (-0.5)
    value_part = jnp.einsum(
        "hqk,qhd->khd", prob_weights, head_grads, preferred_element_type=jnp.float32
    )
    row_count = key_part.shape[0]
    return jnp.concatenate(
        [key_part.reshape(row_count, HD), value_part.reshape(row_count, HD)], axis=1
    )


def query_side(queries, head_grads, keys_values, local_rows):
    seq_rows = local_rows * lax.axis_size("seq")
    start_stats = (
        jnp.full((HEADS, local_rows), -1e30, jnp.float32),
        jnp.zeros((HEADS, local_rows), jnp.float32),
        jnp.zeros((HEADS, local_rows), jnp.float32),
    )
    all_pairs = lax.all_gather(keys_values, "seq", axis=0, tiled=True)
    statistics = update_stats(start_stats, queries, head_grads, all_pairs)
    row_max, row_total, row_mix = statistics
    log_total = row_max + jnp.log(row_total)
    row_delta = row_mix / row_total
    sub_size = math.gcd(seq_rows, 512)
    block_count = seq_rows // sub_size
    empty_query = jnp.zeros((local_rows, HEADS, HEAD_DIM), jnp.float32)

    def backward_step(block_index, running):
        query_grad, buffer = running
        pair_block = lax.dynamic_slice_in_dim(all_pairs, block_index * sub_size, sub_size, 0)
        keys_blk, prob_weights, dscore = block_backward(
            queries, head_grads, pair_block, log_total, row_delta
        )
        query_grad = query_grad + jnp.einsum(
            "hqk,khd->qhd", dscore, keys_blk, preferred_element_type=jnp.float32
        )
        block_terms = key_terms_from(queries, head_grads, prob_weights, dscore)
        buffer = lax.dynamic_update_slice_in_dim(buffer, block_terms, block_index * sub_size, 0)
        return (query_grad, buffer)

    empty_terms = jnp.zeros((seq_rows, 2 * HD), jnp.float32)
    query_grad, buffer = lax.fori_loop(0, block_count, backward_step, (empty_query, empty_terms))
    pair_grads = lax.psum_scatter(
        buffer.astype(jnp.bfloat16), "seq", scatter_dimension=0, tiled=True
    ).astype(jnp.float32)
    return (query_grad, pair_grads)


def general(
    tokens,
    upstream_grad,
    norm_gain,
    norm_bias,
    input_codes,
    input_scales,
    input_bias,
    output_codes,
    output_scales,
    layer_scale,
):
    all_codes, all_scales = (
        lax.all_gather(input_codes.astype(jnp.float32), "weight", axis=0, tiled=True).astype(
            input_codes.dtype
        ),
        lax.all_gather(input_scales, "weight", axis=0, tiled=True),
    )
    input_weight = dequantize(all_codes, all_scales)
    output_weight = dequantize(output_codes, output_scales)
    normed, inverse, norm_out = normalize(tokens[0].astype(jnp.float32), norm_gain, norm_bias)
    projected = (
        jnp.dot(norm_out, input_weight, preferred_element_type=jnp.float32) + input_bias
    ).astype(jnp.bfloat16)
    local_rows = projected.shape[0]
    queries = projected[:, :HD].reshape(local_rows, HEADS, HEAD_DIM)
    keys_values = projected[:, HD:]
    scaled_grad = (upstream_grad[0].astype(jnp.float32) * layer_scale).astype(jnp.bfloat16)
    head_grads = jnp.dot(scaled_grad, output_weight.T, preferred_element_type=jnp.float32).astype(
        jnp.bfloat16
    )
    head_grads = head_grads.reshape(local_rows, HEADS, HEAD_DIM)
    query_grad, pair_grads = query_side(queries, head_grads, keys_values, local_rows)
    query_grad = (query_grad * HEAD_DIM ** (-0.5)).reshape(local_rows, HD)
    grad_proj = jnp.concatenate([query_grad, pair_grads], axis=1).astype(jnp.bfloat16)
    grad_norm = jnp.dot(grad_proj, input_weight.T, preferred_element_type=jnp.float32)
    result = norm_backward(grad_norm, normed, inverse, norm_gain)
    return result[None]


WIDTH = 1536
ROWS = 128
SHARD = 384
HALF = 384
GROUP = 192
BF16 = jnp.bfloat16
F32 = jnp.float32
MESH = pl.DeviceIdType.MESH
NT = (((1,), (1,)), ((), ()))


def fits(mesh):
    return dict(mesh.shape) == {"groups": 2, "seq": 4, "weight": 4}


def fused_kernel(
    tokens_hbm,
    upstream_hbm,
    gain_hbm,
    norm_bias_hbm,
    codes_hbm,
    in_scales_hbm,
    in_bias_hbm,
    out_codes_hbm,
    out_scales_hbm,
    layer_scale_hbm,
    out_ref,
    gain_ref,
    norm_bias_ref,
    in_scales,
    in_bias_ref,
    out_scales,
    layer_scale_ref,
    weight,
    codes,
    out_codes,
    out_weight,
    tokens,
    upstream,
    normed_buf,
    inverse_buf,
    norm_out,
    scaled,
    packed,
    gathered,
    grads,
    grad_proj,
    load_sem,
    w_send,
    w_recv,
    a_send,
    a_recv,
    g_send,
    g_recv,
):
    g = lax.axis_index("groups")
    s = lax.axis_index("seq")
    w = lax.axis_index("weight")
    core = lax.rem(w, 2)
    across = lax.rem(w + 2, 4)
    sibling = w + 1 - 2 * core
    far_sibling = lax.rem(sibling + 2, 4)
    near = s // 2
    far = 1 - near
    buddy = s + 1 - 2 * lax.rem(s, 2)
    parity = lax.rem(s, 2)

    def load(index, source, target):
        copy = pltpu.make_async_copy(source, target, load_sem.at[index])
        copy.start()
        return copy

    load_in_scales = load(4, in_scales_hbm, in_scales)
    load_codes = load(0, codes_hbm, codes)
    load_tokens = load(1, tokens_hbm.at[0], tokens)
    load_upstream = load(2, upstream_hbm.at[0], upstream)
    load_out_codes = load(3, out_codes_hbm, out_codes)
    load_out_scales = load(5, out_scales_hbm, out_scales)
    load_layer_scale = load(6, layer_scale_hbm, layer_scale_ref)
    load_gain = load(7, gain_hbm, gain_ref)
    load_norm_bias = load(8, norm_bias_hbm, norm_bias_ref)
    load_in_bias = load(9, in_bias_hbm, in_bias_ref)

    barrier = pltpu.get_barrier_semaphore()
    peers = [{"weight": across}, {"weight": sibling}, {"groups": 1 - g}]
    peers += [{"seq": lax.rem(s + k, 4)} for k in (1, 2, 3)]
    for peer in peers:
        pl.semaphore_signal(barrier, inc=1, device_id=peer, device_id_type=MESH)

    def half_of(j):
        return far if j < 3 else near

    def columns_of(j):
        return pl.ds(pl.multiple_of(768 * (j % 3) + HALF * half_of(j), 128), HALF)

    def dequantize_chunk(j):
        first = 6 * (j % 3) + 3 * half_of(j)
        for rb in range(3):
            for cb in range(3):
                cols = pl.ds(pl.multiple_of(128 * (first + cb), 128), 128)
                rows = pl.ds(pl.multiple_of(SHARD * w + 128 * rb, 128), 128)
                block = codes[128 * rb : 128 * (rb + 1), cols].astype(F32)
                weight[rows, cols] = (block * in_scales[rb, first + cb]).astype(BF16)

    def weight_copy(kind, j, row, count, peer):
        part = weight.at[pl.ds(pl.multiple_of(row, 64), count), columns_of(j)]
        return pltpu.make_async_remote_copy(
            src_ref=part,
            dst_ref=part,
            send_sem=w_send.at[kind, j],
            recv_sem=w_recv.at[kind, j],
            device_id=peer,
            device_id_type=MESH,
        )

    def x_copy(j, owner):
        return weight_copy(0, j, SHARD * owner + GROUP * g, GROUP, {"weight": across})

    def y_copy(j, part):
        return weight_copy(1, j, SHARD * across + GROUP * part, GROUP, {"groups": 1 - g})

    def own_copy(j, owner):
        return weight_copy(2, j, SHARD * owner, SHARD, {"weight": sibling})

    def passed_copy(j, owner):
        return weight_copy(3, j, SHARD * owner, SHARD, {"weight": sibling})

    def start_own(j):
        x_copy(j, w).start()
        own_copy(j, w).start()

    def exchange(t, dest, send_index, recv_index):
        return pltpu.make_async_remote_copy(
            src_ref=packed.at[t, pl.ds(pl.multiple_of(GROUP * dest, 64), GROUP), :],
            dst_ref=gathered.at[t, s],
            send_sem=a_send.at[t, send_index],
            recv_sem=a_recv.at[t, recv_index],
            device_id={"seq": dest},
            device_id_type=MESH,
        )

    def exchange_done(t, source, index):
        return pltpu.make_async_remote_copy(
            src_ref=packed.at[t, pl.ds(pl.multiple_of(GROUP * source, 64), GROUP), :],
            dst_ref=gathered.at[t, source],
            send_sem=a_send.at[t, index],
            recv_sem=a_recv.at[t, index],
            device_id={"seq": source},
            device_id_type=MESH,
        )

    def share(t, is_far, value):
        half = far if is_far else near
        packed[t, pl.ds(pl.multiple_of(HALF * half, 128), HALF), :] = value
        if is_far:
            for k in range(2):
                exchange(t, 2 * far + k, k, parity).start()
        else:
            exchange(t, buddy, 2, 2).start()
            gathered[t, s] = packed[t, pl.ds(pl.multiple_of(GROUP * s, 64), GROUP), :]

    def head_gradients(is_far):
        half = far if is_far else near
        for rb in range(3):
            rows = pl.ds(pl.multiple_of(HALF * half + 128 * rb, 128), 128)
            for cb in range(12):
                block = out_codes[rows, 128 * cb : 128 * (cb + 1)].astype(F32)
                out_weight[128 * rb : 128 * (rb + 1), 128 * cb : 128 * (cb + 1)] = (
                    block * out_scales[3 * half + rb, cb]
                ).astype(BF16)
        value = lax.dot_general(out_weight[...], scaled[...], NT, preferred_element_type=F32)
        share(3, is_far, value.astype(BF16))

    def project(j):
        value = jnp.dot(norm_out[...], weight[:, columns_of(j)], preferred_element_type=F32)
        value = value + in_bias_ref[columns_of(j)][None]
        if j % 3 == 0:
            value = value * HEAD_DIM ** (-0.5)
        share(j % 3, j < 3, value.T.astype(BF16))

    load_in_scales.wait()
    load_codes.wait()
    dequantize_chunk(0)
    dequantize_chunk(1)
    pl.semaphore_wait(barrier, 6)
    start_own(0)
    start_own(1)
    for j in range(2, 6):
        dequantize_chunk(j)

    load_layer_scale.wait()
    load_upstream.wait()
    scaled[...] = (upstream[...].astype(F32) * layer_scale_ref[...][None]).astype(BF16)
    load_out_scales.wait()
    load_out_codes.wait()
    head_gradients(True)

    load_gain.wait()
    load_norm_bias.wait()
    load_in_bias.wait()
    load_tokens.wait()
    normed, inverse, rounded = normalize(
        tokens[...].astype(F32), gain_ref[...][None], norm_bias_ref[...][None]
    )
    normed_buf[...] = normed
    inverse_buf[...] = inverse
    norm_out[...] = rounded

    for step in range(8):
        if step < 6:
            x_copy(step, across).wait_recv()
            if step + 2 < 6:
                start_own(step + 2)
            y_copy(step, g).start()
        if 1 <= step < 7:
            y_copy(step - 1, 1 - g).wait_recv()
            passed_copy(step - 1, across).start()
        if step == 0:
            head_gradients(False)
        if step >= 2:
            own_copy(step - 2, sibling).wait_recv()
            passed_copy(step - 2, far_sibling).wait_recv()
            project(step - 2)

    for t in (0, 1, 2, 3):
        for k in range(2):
            exchange_done(t, 2 * far + k, k).wait_recv()
        exchange_done(t, buddy, 2).wait_recv()

    def grad_copy(h, dest, source, send_index, recv_index, peer):
        rows = pl.ds(pl.multiple_of(GROUP * source + HEAD_DIM * h, 64), HEAD_DIM)
        return pltpu.make_async_remote_copy(
            src_ref=grads.at[h, dest],
            dst_ref=grad_proj.at[:, rows, :],
            send_sem=g_send.at[h, send_index],
            recv_sem=g_recv.at[h, recv_index],
            device_id={"seq": peer},
            device_id_type=MESH,
        )

    for h in range(3):
        rows = slice(HEAD_DIM * h, HEAD_DIM * (h + 1))
        q_t, k_t, v_t, g_t = (
            jnp.concatenate([gathered[t, i, rows, :] for i in range(4)], axis=1) for t in range(4)
        )
        scores = jnp.dot(k_t.T, q_t, preferred_element_type=F32)
        dprob = jnp.dot(v_t.T, g_t, preferred_element_type=F32)
        expo = jnp.exp(scores - jnp.max(scores, axis=0, keepdims=True))
        probs = expo * (1.0 / jnp.sum(expo, axis=0, keepdims=True))
        delta = jnp.sum(probs * dprob, axis=0, keepdims=True)
        dscore = (probs * (dprob - delta)).astype(BF16)
        parts = (
            jnp.dot(k_t, dscore, preferred_element_type=F32) * HEAD_DIM ** (-0.5),
            lax.dot_general(q_t, dscore, NT, preferred_element_type=F32),
            lax.dot_general(g_t, probs.astype(BF16), NT, preferred_element_type=F32),
        )
        for t in range(3):
            value = parts[t].astype(BF16)
            for i in range(4):
                grads[h, i, t] = value[:, ROWS * i : ROWS * (i + 1)]
        for k in range(2):
            grad_copy(h, 2 * far + k, s, k, parity, 2 * far + k).start()
        grad_copy(h, buddy, s, 2, 2, buddy).start()
        own = pl.ds(pl.multiple_of(GROUP * s + HEAD_DIM * h, 64), HEAD_DIM)
        grad_proj[:, own, :] = grads[h, s]

    def back(half):
        total = None
        for t in range(3):
            rows = pl.ds(pl.multiple_of(HALF * half, 128), HALF)
            cols = pl.ds(pl.multiple_of(768 * t + HALF * half, 128), HALF)
            term = lax.dot_general(
                grad_proj[t, rows, :].T, weight[:, cols], NT, preferred_element_type=F32
            )
            total = term if total is None else total + term
        return total

    for h in range(3):
        grad_copy(h, buddy, buddy, 2, 2, buddy).wait_recv()
    out_ref[0] = back(near)
    for h in range(3):
        for k in range(2):
            grad_copy(h, 2 * far + k, 2 * far + k, k, k, 2 * far + k).wait_recv()
    grad_norm = out_ref[0] + back(far)
    out_ref[0] = norm_backward(grad_norm, normed_buf[...], inverse_buf[...], gain_ref[...][None])

    for j in range(6):
        x_copy(j, w).wait_send()
        own_copy(j, w).wait_send()
        y_copy(j, g).wait_send()
        passed_copy(j, across).wait_send()
    for t in range(4):
        for k in range(2):
            exchange(t, 2 * far + k, k, parity).wait_send()
        exchange(t, buddy, 2, 2).wait_send()
    for h in range(3):
        for k in range(2):
            grad_copy(h, 2 * far + k, s, k, parity, 2 * far + k).wait_send()
        grad_copy(h, buddy, s, 2, 2, buddy).wait_send()


def fused(
    tokens,
    upstream_grad,
    norm_gain,
    norm_bias,
    input_codes,
    input_scales,
    input_bias,
    output_codes,
    output_scales,
    layer_scale,
):
    hbm = pl.BlockSpec(memory_space=pltpu.HBM)
    vmem = pl.BlockSpec(memory_space=pltpu.VMEM)
    return pl.pallas_call(
        fused_kernel,
        out_shape=jax.ShapeDtypeStruct((1, ROWS, WIDTH), F32),
        in_specs=[hbm] * 10,
        out_specs=vmem,
        scratch_shapes=[
            pltpu.VMEM((WIDTH,), F32),
            pltpu.VMEM((WIDTH,), F32),
            pltpu.SMEM((3, 18), F32),
            pltpu.VMEM((3 * HD,), F32),
            pltpu.SMEM((6, 12), F32),
            pltpu.VMEM((WIDTH,), F32),
            pltpu.VMEM((WIDTH, 3 * HD), BF16),
            pltpu.VMEM((SHARD, 3 * HD), BF16),
            pltpu.VMEM((HD, WIDTH), BF16),
            pltpu.VMEM((HALF, WIDTH), BF16),
            pltpu.VMEM((ROWS, WIDTH), BF16),
            pltpu.VMEM((ROWS, WIDTH), BF16),
            pltpu.VMEM((ROWS, WIDTH), F32),
            pltpu.VMEM((ROWS, 1), F32),
            pltpu.VMEM((ROWS, WIDTH), BF16),
            pltpu.VMEM((ROWS, WIDTH), BF16),
            pltpu.VMEM((4, HD, ROWS), BF16),
            pltpu.VMEM((4, 4, GROUP, ROWS), BF16),
            pltpu.VMEM((3, 4, 3, HEAD_DIM, ROWS), BF16),
            pltpu.VMEM((3, HD, ROWS), BF16),
            pltpu.SemaphoreType.DMA((10,)),
            pltpu.SemaphoreType.DMA((4, 6)),
            pltpu.SemaphoreType.DMA((4, 6)),
            pltpu.SemaphoreType.DMA((4, 3)),
            pltpu.SemaphoreType.DMA((4, 3)),
            pltpu.SemaphoreType.DMA((3, 3)),
            pltpu.SemaphoreType.DMA((3, 3)),
        ],
        compiler_params=pltpu.CompilerParams(
            collective_id=0, has_side_effects=True, vmem_limit_bytes=64 * 1024 * 1024 - 65536
        ),
        cost_estimate=pl.CostEstimate(
            flops=2500000000, bytes_accessed=8000000, transcendentals=1000000
        ),
    )(
        tokens,
        upstream_grad,
        norm_gain,
        norm_bias,
        input_codes,
        input_scales,
        input_bias,
        output_codes,
        output_scales,
        layer_scale,
    )


def solution(mesh):
    in_specs = (
        P(("groups", "weight"), "seq", None),
        P(("groups", "weight"), "seq", None),
        P(),
        P(),
        P("weight", None),
        P("weight", None),
        P(),
        P(),
        P(),
        P(),
    )
    out_specs = P(("groups", "weight"), "seq", None)
    local = fused if fits(mesh) else general
    return jax.shard_map(local, mesh=mesh, in_specs=in_specs, out_specs=out_specs, check_vma=False)
```

profile of v0, /device:TPU:1, one launch (start us, length us, event | category | flops | bytes accessed | tf_op | source)
XLA Modules:
  0.0 55.6 jit_solution(2424647304266878888)
XLA Ops:
  0.0 53.5 %shard_map.100 = f32[1,128,1536]{2,1,0:T(8,128)} custom-call(bf16[1,128,1536]{2,1,0:T(8,128)(2,1)} %tokens_hbm.1, bf16[1,128,1536]{2,1,0:T(8,128)(2,1)} %upstream_hbm.1, f32[1536]{0:T(1024)} %gain_hbm.1, f32[1536]{0:T(1024)} %norm_bias_hbm.1, bf16[384,2304]{1,0:T(8,128)(2,1)} %codes_hbm.1, f32[3,18]{1,0:T(4,128)} %in_scales_hbm.1, f32[2304]{0:T(1024)} %in_bias_hbm.1, ...), custom_call_target="tpu_custom_call" | custom-call | flops 2500000000 | bytes 8000000 | tf_op jit(solution)/shard_map/pallas_call | solution.py:481
  53.5 2.1 %copy.12 = f32[1,128,1536]{2,1,0:T(8,128)} copy(f32[1,128,1536]{2,1,0:T(8,128)} %shard_map.100) | data formatting | bytes 1572864
where the time goes:
time: 56.7 us; the launch traced here: 55.6 us
  Pallas kernels  53.5 us (94%)
  local copies, waits for them, and re-layouts  2.07 us (4%)
    pallas_call x1, Pallas kernels, fused(): pl.pallas_call(fused_kernel, out_shape=jax.ShapeDtypeStruct((1, ROWS, WID...  53.5 us
    unnamed x1, local copies, waits for them, and re-layouts  2.07 us

commit v1 on v0

--- a/solution.py
+++ b/solution.py
@@ -168,6 +168,8 @@
 SHARD = 384
 HALF = 384
 GROUP = 192
+PARTS = 2
+PART = ROWS // PARTS
 BF16 = jnp.bfloat16
 F32 = jnp.float32
 MESH = pl.DeviceIdType.MESH
@@ -204,15 +206,20 @@
     upstream,
     normed_buf,
     inverse_buf,
+    raw,
     norm_out,
     scaled,
     packed,
     gathered,
+    projected,
     grads,
     grad_proj,
     load_sem,
     w_send,
     w_recv,
+    t_send,
+    p_send,
+    t_recv,
     a_send,
     a_recv,
     g_send,
@@ -225,10 +232,13 @@
     across = lax.rem(w + 2, 4)
     sibling = w + 1 - 2 * core
     far_sibling = lax.rem(sibling + 2, 4)
-    near = s // 2
-    far = 1 - near
-    buddy = s + 1 - 2 * lax.rem(s, 2)
-    parity = lax.rem(s, 2)
+    side = s // 2
+    half = lax.rem(s, 2)
+    home = core == side
+    inner = lax.rem(s + side, 2) == 1
+    owner = w - core + side
+    place = 2 * half + core
+    blocks = (s, s + 1 - 2 * half, 2 - side, 3 - 3 * side)
 
     def load(index, source, target):
         copy = pltpu.make_async_copy(source, target, load_sem.at[index])
@@ -237,9 +247,9 @@
 
     load_in_scales = load(4, in_scales_hbm, in_scales)
     load_codes = load(0, codes_hbm, codes)
-    load_tokens = load(1, tokens_hbm.at[0], tokens)
     load_upstream = load(2, upstream_hbm.at[0], upstream)
     load_out_codes = load(3, out_codes_hbm, out_codes)
+    load_tokens = load(1, tokens_hbm.at[0], tokens)
     load_out_scales = load(5, out_scales_hbm, out_scales)
     load_layer_scale = load(6, layer_scale_hbm, layer_scale_ref)
     load_gain = load(7, gain_hbm, gain_ref)
@@ -248,12 +258,24 @@
 
     barrier = pltpu.get_barrier_semaphore()
     peers = [{"weight": across}, {"weight": sibling}, {"groups": 1 - g}]
-    peers += [{"seq": lax.rem(s + k, 4)} for k in (1, 2, 3)]
+    for k in (1, 2, 3):
+        peers.append({"seq": lax.rem(s + k, 4)})
+        peers.append({"seq": lax.rem(s + k, 4), "weight": sibling})
     for peer in peers:
         pl.semaphore_signal(barrier, inc=1, device_id=peer, device_id_type=MESH)
 
+    def remote(source, target, send, recv, peer):
+        return pltpu.make_async_remote_copy(
+            src_ref=source,
+            dst_ref=target,
+            send_sem=send,
+            recv_sem=recv,
+            device_id=peer,
+            device_id_type=MESH,
+        )
+
     def half_of(j):
-        return far if j < 3 else near
+        return half if j < 3 else 1 - half
 
     def columns_of(j):
         return pl.ds(pl.multiple_of(768 * (j % 3) + HALF * half_of(j), 128), HALF)
@@ -269,86 +291,145 @@
 
     def weight_copy(kind, j, row, count, peer):
         part = weight.at[pl.ds(pl.multiple_of(row, 64), count), columns_of(j)]
-        return pltpu.make_async_remote_copy(
-            src_ref=part,
-            dst_ref=part,
-            send_sem=w_send.at[kind, j],
-            recv_sem=w_recv.at[kind, j],
-            device_id=peer,
-            device_id_type=MESH,
-        )
-
-    def x_copy(j, owner):
-        return weight_copy(0, j, SHARD * owner + GROUP * g, GROUP, {"weight": across})
+        return remote(part, part, w_send.at[kind, j], w_recv.at[kind, j], peer)
+
+    def x_copy(j, shard):
+        return weight_copy(0, j, SHARD * shard + GROUP * g, GROUP, {"weight": across})
 
     def y_copy(j, part):
         return weight_copy(1, j, SHARD * across + GROUP * part, GROUP, {"groups": 1 - g})
 
-    def own_copy(j, owner):
-        return weight_copy(2, j, SHARD * owner, SHARD, {"weight": sibling})
-
-    def passed_copy(j, owner):
-        return weight_copy(3, j, SHARD * owner, SHARD, {"weight": sibling})
+    def own_copy(j, shard):
+        return weight_copy(2, j, SHARD * shard, SHARD, {"weight": sibling})
+
+    def passed_copy(j, shard):
+        return weight_copy(3, j, SHARD * shard, SHARD, {"weight": sibling})
 
     def start_own(j):
         x_copy(j, w).start()
         own_copy(j, w).start()
 
-    def exchange(t, dest, send_index, recv_index):
-        return pltpu.make_async_remote_copy(
-            src_ref=packed.at[t, pl.ds(pl.multiple_of(GROUP * dest, 64), GROUP), :],
-            dst_ref=gathered.at[t, s],
-            send_sem=a_send.at[t, send_index],
-            recv_sem=a_recv.at[t, recv_index],
-            device_id={"seq": dest},
-            device_id_type=MESH,
-        )
-
-    def exchange_done(t, source, index):
-        return pltpu.make_async_remote_copy(
-            src_ref=packed.at[t, pl.ds(pl.multiple_of(GROUP * source, 64), GROUP), :],
-            dst_ref=gathered.at[t, source],
-            send_sem=a_send.at[t, index],
-            recv_sem=a_recv.at[t, index],
-            device_id={"seq": source},
-            device_id_type=MESH,
-        )
-
-    def share(t, is_far, value):
-        half = far if is_far else near
-        packed[t, pl.ds(pl.multiple_of(HALF * half, 128), HALF), :] = value
-        if is_far:
-            for k in range(2):
-                exchange(t, 2 * far + k, k, parity).start()
-        else:
-            exchange(t, buddy, 2, 2).start()
-            gathered[t, s] = packed[t, pl.ds(pl.multiple_of(GROUP * s, 64), GROUP), :]
-
-    def head_gradients(is_far):
-        half = far if is_far else near
+    def from_x(j):
+        x_copy(j, across).wait_recv()
+        y_copy(j, g).start()
+
+    def from_y(j):
+        y_copy(j, 1 - g).wait_recv()
+        passed_copy(j, across).start()
+
+    def weight_ready(j):
+        own_copy(j, sibling).wait_recv()
+        passed_copy(j, far_sibling).wait_recv()
+
+    def part_rows(part):
+        return pl.ds(PART * part, PART)
+
+    def send_tokens(part):
+        dest = jnp.where(home & inner, 3 * core, 1 + core)
+        return remote(
+            tokens_hbm.at[0, part_rows(part)],
+            raw.at[s, part_rows(part)],
+            t_send.at[0, part],
+            t_recv.at[s, part],
+            {"seq": dest},
+        )
+
+    def forward_tokens(slot, part):
+        z = blocks[slot]
+        rows = raw.at[z, part_rows(part)]
+        return remote(
+            rows, rows, t_send.at[slot - 1, part], t_recv.at[z, part], {"seq": 3 * core}
+        )
+
+    def pass_tokens(slot, part):
+        z = blocks[slot]
+        rows = raw.at[z, part_rows(part)]
+        source = tokens_hbm.at[0, part_rows(part)] if slot == 0 else rows
+        return remote(source, rows, p_send.at[slot, part], t_recv.at[z, part], {"weight": sibling})
+
+    def tokens_here(slot, part):
+        pass_tokens(slot, part).wait_recv()
+
+    def relay(slot, part, forward):
+        tokens_here(slot, part)
+        if forward:
+            forward_tokens(slot, part).start()
+        pass_tokens(slot, part).start()
+
+    def share(q):
+        peer = {"seq": 2 * core + q // 2, "weight": w - core + q % 2}
+        return remote(
+            packed.at[GROUP * q : GROUP * (q + 1), :],
+            gathered.at[s],
+            a_send.at[q],
+            a_recv.at[s],
+            peer,
+        )
+
+    def share_done(z):
+        return remote(
+            packed.at[0:GROUP, :],
+            gathered.at[z],
+            a_send.at[0],
+            a_recv.at[z],
+            {"weight": sibling},
+        )
+
+    def stays(q):
+        return home & (place == q)
+
+    def head_gradients(part):
         for rb in range(3):
-            rows = pl.ds(pl.multiple_of(HALF * half + 128 * rb, 128), 128)
+            rows = slice(HALF * part + 128 * rb, HALF * part + 128 * (rb + 1))
             for cb in range(12):
-                block = out_codes[rows, 128 * cb : 128 * (cb + 1)].astype(F32)
-                out_weight[128 * rb : 128 * (rb + 1), 128 * cb : 128 * (cb + 1)] = (
-                    block * out_scales[3 * half + rb, cb]
+                cols = slice(128 * cb, 128 * (cb + 1))
+                block = out_codes[rows, cols].astype(F32)
+                out_weight[128 * rb : 128 * (rb + 1), cols] = (
+                    block * out_scales[3 * part + rb, cb]
                 ).astype(BF16)
         value = lax.dot_general(out_weight[...], scaled[...], NT, preferred_element_type=F32)
-        share(3, is_far, value.astype(BF16))
-
-    def project(j):
-        value = jnp.dot(norm_out[...], weight[:, columns_of(j)], preferred_element_type=F32)
-        value = value + in_bias_ref[columns_of(j)][None]
-        if j % 3 == 0:
+        packed[HALF * part : HALF * (part + 1), :] = value.astype(BF16)
+        for q in (2 * part, 2 * part + 1):
+
+            @pl.when(jnp.logical_not(stays(q)))
+            def _():
+                share(q).start()
+
+            @pl.when(stays(q))
+            def _():
+                gathered[s] = packed[GROUP * q : GROUP * (q + 1), :]
+
+    def normalize_slot(slot):
+        norm_out[ROWS * slot : ROWS * (slot + 1), :] = normalize(
+            raw[blocks[slot]].astype(F32), gain_ref[...][None], norm_bias_ref[...][None]
+        )[2]
+
+    def project(t, pair):
+        first = pl.multiple_of(768 * t + HALF * half + 128 * core, 128)
+        value = jnp.dot(
+            norm_out[256 * pair : 256 * (pair + 1), :],
+            weight[:, pl.ds(first, 256)],
+            preferred_element_type=F32,
+        )
+        value = value + in_bias_ref[pl.ds(first, 256)][None]
+        if t == 0:
             value = value * HEAD_DIM ** (-0.5)
-        share(j % 3, j < 3, value.T.astype(BF16))
+        projected[t, :, 256 * pair : 256 * (pair + 1)] = value.T.astype(BF16)
 
     load_in_scales.wait()
     load_codes.wait()
     dequantize_chunk(0)
+    pl.semaphore_wait(barrier, len(peers))
+    for part in range(PARTS):
+        send_tokens(part).start()
+    start_own(0)
+
+    @pl.when(home)
+    def _():
+        for part in range(PARTS):
+            pass_tokens(0, part).start()
+
     dequantize_chunk(1)
-    pl.semaphore_wait(barrier, 6)
-    start_own(0)
     start_own(1)
     for j in range(2, 6):
         dequantize_chunk(j)
@@ -358,7 +439,8 @@
     scaled[...] = (upstream[...].astype(F32) * layer_scale_ref[...][None]).astype(BF16)
     load_out_scales.wait()
     load_out_codes.wait()
-    head_gradients(True)
+    head_gradients(0)
+    head_gradients(1)
 
     load_gain.wait()
     load_norm_bias.wait()
@@ -369,44 +451,119 @@
     )
     normed_buf[...] = normed
     inverse_buf[...] = inverse
-    norm_out[...] = rounded
-
-    for step in range(8):
-        if step < 6:
-            x_copy(step, across).wait_recv()
-            if step + 2 < 6:
-                start_own(step + 2)
-            y_copy(step, g).start()
-        if 1 <= step < 7:
-            y_copy(step - 1, 1 - g).wait_recv()
-            passed_copy(step - 1, across).start()
-        if step == 0:
-            head_gradients(False)
-        if step >= 2:
-            own_copy(step - 2, sibling).wait_recv()
-            passed_copy(step - 2, far_sibling).wait_recv()
-            project(step - 2)
-
-    for t in (0, 1, 2, 3):
-        for k in range(2):
-            exchange_done(t, 2 * far + k, k).wait_recv()
-        exchange_done(t, buddy, 2).wait_recv()
-
-    def grad_copy(h, dest, source, send_index, recv_index, peer):
-        rows = pl.ds(pl.multiple_of(GROUP * source + HEAD_DIM * h, 64), HEAD_DIM)
-        return pltpu.make_async_remote_copy(
-            src_ref=grads.at[h, dest],
-            dst_ref=grad_proj.at[:, rows, :],
-            send_sem=g_send.at[h, send_index],
-            recv_sem=g_recv.at[h, recv_index],
-            device_id={"seq": peer},
-            device_id_type=MESH,
-        )
+
+    @pl.when(home)
+    def _():
+        norm_out[0:ROWS, :] = rounded
+
+    from_x(0)
+    start_own(2)
+
+    @pl.when(home)
+    def _():
+        for part in range(PARTS):
+            relay(1, part, False)
+
+    @pl.when(home & inner)
+    def _():
+        for slot in (2, 3):
+            relay(slot, 0, True)
+
+    from_x(1)
+    from_y(0)
+
+    @pl.when(jnp.logical_not(home))
+    def _():
+        for slot in (0, 1):
+            for part in range(PARTS):
+                tokens_here(slot, part)
+        normalize_slot(0)
+
+    normalize_slot(1)
+
+    @pl.when(home & inner)
+    def _():
+        for part in range(1, PARTS):
+            for slot in (2, 3):
+                relay(slot, part, True)
+
+    from_x(2)
+    start_own(3)
+    start_own(4)
+    from_y(1)
+    weight_ready(0)
+    project(0, 0)
+
+    @pl.when(inner)
+    def _():
+        @pl.when(jnp.logical_not(home))
+        def _():
+            for slot in (2, 3):
+                for part in range(PARTS):
+                    tokens_here(slot, part)
+
+        normalize_slot(2)
+        normalize_slot(3)
+        project(0, 1)
+
+    weight_ready(1)
+    project(1, 0)
+    from_y(2)
+
+    @pl.when(inner)
+    def _():
+        project(1, 1)
+
+    weight_ready(2)
+    project(2, 0)
+
+    @pl.when(inner)
+    def _():
+        project(2, 1)
+
+    @pl.when(jnp.logical_not(inner))
+    def _():
+        @pl.when(home)
+        def _():
+            for part in range(PARTS):
+                for slot in (2, 3):
+                    relay(slot, part, False)
+
+        @pl.when(jnp.logical_not(home))
+        def _():
+            for part in range(PARTS):
+                for slot in (2, 3):
+                    tokens_here(slot, part)
+
+        normalize_slot(2)
+        normalize_slot(3)
+        for t in range(3):
+            project(t, 1)
+
+    for z in range(4):
+
+        @pl.when(jnp.logical_not(home & (s == z)))
+        def _():
+            share_done(z).wait_recv()
+
+    def grad_copy(h, slot, q, peer):
+        rows = pl.ds(pl.multiple_of(GROUP * q + HEAD_DIM * h, 64), HEAD_DIM)
+        return remote(
+            grads.at[h, slot],
+            grad_proj.at[:, rows, :],
+            g_send.at[h, slot],
+            g_recv.at[h, q],
+            peer,
+        )
+
+    def send_grads(h, slot):
+        return grad_copy(h, slot, place, {"seq": blocks[slot], "weight": owner})
 
     for h in range(3):
-        rows = slice(HEAD_DIM * h, HEAD_DIM * (h + 1))
-        q_t, k_t, v_t, g_t = (
-            jnp.concatenate([gathered[t, i, rows, :] for i in range(4)], axis=1) for t in range(4)
+        mine = pl.ds(pl.multiple_of(HEAD_DIM * core + HEAD_DIM * h, 64), HEAD_DIM)
+        q_t, k_t, v_t = (projected[t, mine, :] for t in range(3))
+        g_t = jnp.concatenate(
+            [gathered[z, HEAD_DIM * h : HEAD_DIM * (h + 1), :] for z in blocks], axis=1
         )
         scores = jnp.dot(k_t.T, q_t, preferred_element_type=F32)
         dprob = jnp.dot(v_t.T, g_t, preferred_element_type=F32)
@@ -423,30 +580,51 @@
             value = parts[t].astype(BF16)
             for i in range(4):
                 grads[h, i, t] = value[:, ROWS * i : ROWS * (i + 1)]
-        for k in range(2):
-            grad_copy(h, 2 * far + k, s, k, parity, 2 * far + k).start()
-        grad_copy(h, buddy, s, 2, 2, buddy).start()
-        own = pl.ds(pl.multiple_of(GROUP * s + HEAD_DIM * h, 64), HEAD_DIM)
-        grad_proj[:, own, :] = grads[h, s]
-
-    def back(half):
+        for slot in (3, 2, 1):
+            send_grads(h, slot).start()
+
+        @pl.when(home)
+        def _():
+            own = pl.ds(pl.multiple_of(GROUP * place + HEAD_DIM * h, 64), HEAD_DIM)
+            grad_proj[:, own, :] = grads[h, 0]
+
+        @pl.when(jnp.logical_not(home))
+        def _():
+            send_grads(h, 0).start()
+
+        from_x(3 + h)
+        if h == 0:
+            start_own(5)
+        if h > 0:
+            from_y(2 + h)
+    from_y(5)
+    for j in range(3, 6):
+        weight_ready(j)
+
+    def grads_ready(part):
+        for h in range(3):
+            for k in range(2):
+                q = 2 * part + k
+
+                @pl.when(jnp.logical_not(home & (place == q)))
+                def _():
+                    grad_copy(h, 0, q, {"weight": sibling}).wait_recv()
+
+    def back(part):
         total = None
         for t in range(3):
-            rows = pl.ds(pl.multiple_of(HALF * half, 128), HALF)
-            cols = pl.ds(pl.multiple_of(768 * t + HALF * half, 128), HALF)
+            rows = pl.ds(pl.multiple_of(HALF * part, 128), HALF)
+            cols = pl.ds(pl.multiple_of(768 * t + HALF * part, 128), HALF)
             term = lax.dot_general(
                 grad_proj[t, rows, :].T, weight[:, cols], NT, preferred_element_type=F32
             )
             total = term if total is None else total + term
         return total
 
-    for h in range(3):
-        grad_copy(h, buddy, buddy, 2, 2, buddy).wait_recv()
-    out_ref[0] = back(near)
-    for h in range(3):
-        for k in range(2):
-            grad_copy(h, 2 * far + k, 2 * far + k, k, k, 2 * far + k).wait_recv()
-    grad_norm = out_ref[0] + back(far)
+    grads_ready(1 - core)
+    out_ref[0] = back(1 - core)
+    grads_ready(core)
+    grad_norm = out_ref[0] + back(core)
     out_ref[0] = norm_backward(grad_norm, normed_buf[...], inverse_buf[...], gain_ref[...][None])
 
     for j in range(6):
@@ -454,14 +632,32 @@
         own_copy(j, w).wait_send()
         y_copy(j, g).wait_send()
         passed_copy(j, across).wait_send()
-    for t in range(4):
-        for k in range(2):
-            exchange(t, 2 * far + k, k, parity).wait_send()
-        exchange(t, buddy, 2, 2).wait_send()
+    for part in range(PARTS):
+        send_tokens(part).wait_send()
+
+        @pl.when(home)
+        def _():
+            for slot in range(4):
+                pass_tokens(slot, part).wait_send()
+
+        @pl.when(home & inner)
+        def _():
+            for slot in (2, 3):
+                forward_tokens(slot, part).wait_send()
+
+    for q in range(4):
+
+        @pl.when(jnp.logical_not(stays(q)))
+        def _():
+            share(q).wait_send()
+
     for h in range(3):
-        for k in range(2):
-            grad_copy(h, 2 * far + k, s, k, parity, 2 * far + k).wait_send()
-        grad_copy(h, buddy, s, 2, 2, buddy).wait_send()
+        for slot in (1, 2, 3):
+            send_grads(h, slot).wait_send()
+
+        @pl.when(jnp.logical_not(home))
+        def _():
+            send_grads(h, 0).wait_send()
 
 
 def fused(
@@ -498,19 +694,24 @@
             pltpu.VMEM((ROWS, WIDTH), BF16),
             pltpu.VMEM((ROWS, WIDTH), F32),
             pltpu.VMEM((ROWS, 1), F32),
+            pltpu.VMEM((4, ROWS, WIDTH), BF16),
+            pltpu.VMEM((4 * ROWS, WIDTH), BF16),
             pltpu.VMEM((ROWS, WIDTH), BF16),
-            pltpu.VMEM((ROWS, WIDTH), BF16),
-            pltpu.VMEM((4, HD, ROWS), BF16),
-            pltpu.VMEM((4, 4, GROUP, ROWS), BF16),
+            pltpu.VMEM((HD, ROWS), BF16),
+            pltpu.VMEM((4, GROUP, ROWS), BF16),
+            pltpu.VMEM((3, 256, 4 * ROWS), BF16),
             pltpu.VMEM((3, 4, 3, HEAD_DIM, ROWS), BF16),
             pltpu.VMEM((3, HD, ROWS), BF16),
             pltpu.SemaphoreType.DMA((10,)),
             pltpu.SemaphoreType.DMA((4, 6)),
             pltpu.SemaphoreType.DMA((4, 6)),
-            pltpu.SemaphoreType.DMA((4, 3)),
-            pltpu.SemaphoreType.DMA((4, 3)),
-            pltpu.SemaphoreType.DMA((3, 3)),
-            pltpu.SemaphoreType.DMA((3, 3)),
+            pltpu.SemaphoreType.DMA((3, PARTS)),
+            pltpu.SemaphoreType.DMA((4, PARTS)),
+            pltpu.SemaphoreType.DMA((4, PARTS)),
+            pltpu.SemaphoreType.DMA((4,)),
+            pltpu.SemaphoreType.DMA((4,)),
+            pltpu.SemaphoreType.DMA((3, 4)),
+            pltpu.SemaphoreType.DMA((3, 4)),
         ],
         compiler_params=pltpu.CompilerParams(
             collective_id=0, has_side_effects=True, vmem_limit_bytes=64 * 1024 * 1024 - 65536

time: 56.7 us -> 50.3 us (0.89); the launches traced: 55.6 us -> 50.1 us
  Pallas kernels: 53.5 us -> 48 us
    pallas_call x1, Pallas kernels: 53.5 us -> 48 us  [fused(): pl.pallas_call(fused_kernel, out_shape=jax.ShapeDtypeStruct((1, ROWS, WID...]
where the time goes in v1:
time: 50.3 us; the launch traced here: 50.1 us
  Pallas kernels  48 us (95%)
  local copies, waits for them, and re-layouts  2.07 us (4%)
    pallas_call x1, Pallas kernels, fused(): pl.pallas_call(fused_kernel, out_shape=jax.ShapeDtypeStruct((1, ROWS, WID...  48 us
    unnamed x1, local copies, waits for them, and re-layouts  2.07 us

profile of v1, /device:TPU:1, one launch (start us, length us, event | category | flops | bytes accessed | tf_op | source)
XLA Modules:
  0.0 50.1 jit_solution(12937832560343245096)
XLA Ops:
  0.0 48.0 %shard_map.100 = f32[1,128,1536]{2,1,0:T(8,128)} custom-call(bf16[1,128,1536]{2,1,0:T(8,128)(2,1)} %tokens_hbm.1, bf16[1,128,1536]{2,1,0:T(8,128)(2,1)} %upstream_hbm.1, f32[1536]{0:T(1024)} %gain_hbm.1, f32[1536]{0:T(1024)} %norm_bias_hbm.1, bf16[384,2304]{1,0:T(8,128)(2,1)} %codes_hbm.1, f32[3,18]{1,0:T(4,128)} %in_scales_hbm.1, f32[2304]{0:T(1024)} %in_bias_hbm.1, ...), custom_call_target="tpu_custom_call" | custom-call | flops 2500000000 | bytes 8000000 | tf_op jit(solution)/shard_map/pallas_call | solution.py:677
  48.0 2.1 %copy.12 = f32[1,128,1536]{2,1,0:T(8,128)} copy(f32[1,128,1536]{2,1,0:T(8,128)} %shard_map.100) | data formatting | bytes 1572864

commit v2 on v1

--- a/solution.py
+++ b/solution.py
@@ -168,7 +168,9 @@
 SHARD = 384
 HALF = 384
 GROUP = 192
-PARTS = 2
+CHUNKS = ((0, 0, 192), (0, 192, 192), (1, 0, 192), (1, 192, 192), (2, 0, 192), (2, 192, 192))
+CHUNKS += ((3, 0, 384), (4, 0, 384), (5, 0, 384))
+PARTS = 4
 PART = ROWS // PARTS
 BF16 = jnp.bfloat16
 F32 = jnp.float32
@@ -289,37 +291,47 @@
                 block = codes[128 * rb : 128 * (rb + 1), cols].astype(F32)
                 weight[rows, cols] = (block * in_scales[rb, first + cb]).astype(BF16)
 
-    def weight_copy(kind, j, row, count, peer):
-        part = weight.at[pl.ds(pl.multiple_of(row, 64), count), columns_of(j)]
-        return remote(part, part, w_send.at[kind, j], w_recv.at[kind, j], peer)
-
-    def x_copy(j, shard):
-        return weight_copy(0, j, SHARD * shard + GROUP * g, GROUP, {"weight": across})
-
-    def y_copy(j, part):
-        return weight_copy(1, j, SHARD * across + GROUP * part, GROUP, {"groups": 1 - g})
+    def weight_copy(kind, index, j, row, count, peer):
+        part = weight.at[pl.ds(pl.multiple_of(row, 32), count), columns_of(j)]
+        return remote(part, part, w_send.at[kind, index], w_recv.at[kind, index], peer)
+
+    def x_copy(c, shard):
+        j, first, count = CHUNKS[c]
+        row = SHARD * shard + first + count // 2 * g
+        return weight_copy(0, c, j, row, count // 2, {"weight": across})
+
+    def y_copy(c, part):
+        j, first, count = CHUNKS[c]
+        row = SHARD * across + first + count // 2 * part
+        return weight_copy(1, c, j, row, count // 2, {"groups": 1 - g})
 
     def own_copy(j, shard):
-        return weight_copy(2, j, SHARD * shard, SHARD, {"weight": sibling})
-
-    def passed_copy(j, shard):
-        return weight_copy(3, j, SHARD * shard, SHARD, {"weight": sibling})
+        return weight_copy(2, j, j, SHARD * shard, SHARD, {"weight": sibling})
+
+    def passed_copy(c, shard):
+        j, first, count = CHUNKS[c]
+        return weight_copy(3, c, j, SHARD * shard + first, count, {"weight": sibling})
+
+    def chunks_of(j):
+        return [c for c in range(len(CHUNKS)) if CHUNKS[c][0] == j]
 
     def start_own(j):
-        x_copy(j, w).start()
+        for c in chunks_of(j):
+            x_copy(c, w).start()
         own_copy(j, w).start()
 
-    def from_x(j):
-        x_copy(j, across).wait_recv()
-        y_copy(j, g).start()
-
-    def from_y(j):
-        y_copy(j, 1 - g).wait_recv()
-        passed_copy(j, across).start()
+    def from_x(c):
+        x_copy(c, across).wait_recv()
+        y_copy(c, g).start()
+
+    def from_y(c):
+        y_copy(c, 1 - g).wait_recv()
+        passed_copy(c, across).start()
 
     def weight_ready(j):
         own_copy(j, sibling).wait_recv()
-        passed_copy(j, far_sibling).wait_recv()
+        for c in chunks_of(j):
+            passed_copy(c, far_sibling).wait_recv()
 
     def part_rows(part):
         return pl.ds(PART * part, PART)
@@ -429,10 +441,9 @@
         for part in range(PARTS):
             pass_tokens(0, part).start()
 
-    dequantize_chunk(1)
-    start_own(1)
-    for j in range(2, 6):
+    for j in range(1, 6):
         dequantize_chunk(j)
+        start_own(j)
 
     load_layer_scale.wait()
     load_upstream.wait()
@@ -456,89 +467,81 @@
     def _():
         norm_out[0:ROWS, :] = rounded
 
+    def relay_inner(part):
+        @pl.when(home & inner)
+        def _():
+            relay(2, part, True)
+            relay(3, part, True)
+
+        @pl.when(home)
+        def _():
+            relay(1, part, False)
+
+    def relay_outer(part):
+        @pl.when(home & jnp.logical_not(inner))
+        def _():
+            relay(2, part, False)
+            relay(3, part, False)
+
+    def await_tokens(slots):
+        @pl.when(jnp.logical_not(home))
+        def _():
+            for part in range(PARTS):
+                for slot in slots:
+                    tokens_here(slot, part)
+
     from_x(0)
-    start_own(2)
-
-    @pl.when(home)
-    def _():
-        for part in range(PARTS):
-            relay(1, part, False)
-
-    @pl.when(home & inner)
-    def _():
-        for slot in (2, 3):
-            relay(slot, 0, True)
-
+    relay_inner(0)
     from_x(1)
+    relay_inner(1)
+    from_x(2)
     from_y(0)
+    relay_outer(0)
+    relay_inner(2)
+    from_x(3)
+    from_y(1)
+    relay_outer(1)
+    from_x(4)
+    relay_inner(3)
+    from_y(2)
+    await_tokens((0, 1))
 
     @pl.when(jnp.logical_not(home))
     def _():
-        for slot in (0, 1):
-            for part in range(PARTS):
-                tokens_here(slot, part)
         normalize_slot(0)
 
     normalize_slot(1)
-
-    @pl.when(home & inner)
-    def _():
-        for part in range(1, PARTS):
-            for slot in (2, 3):
-                relay(slot, part, True)
-
-    from_x(2)
-    start_own(3)
-    start_own(4)
-    from_y(1)
+    from_x(5)
+    from_y(3)
+    relay_outer(2)
     weight_ready(0)
     project(0, 0)
 
     @pl.when(inner)
     def _():
-        @pl.when(jnp.logical_not(home))
-        def _():
-            for slot in (2, 3):
-                for part in range(PARTS):
-                    tokens_here(slot, part)
-
+        await_tokens((2, 3))
         normalize_slot(2)
         normalize_slot(3)
         project(0, 1)
 
+    from_y(4)
+    relay_outer(3)
     weight_ready(1)
     project(1, 0)
-    from_y(2)
-
-    @pl.when(inner)
+    from_y(5)
+
+    @pl.when(jnp.logical_not(inner))
     def _():
-        project(1, 1)
-
+        await_tokens((2, 3))
+        normalize_slot(2)
+        normalize_slot(3)
+        project(0, 1)
+
+    project(1, 1)
+    from_x(6)
     weight_ready(2)
     project(2, 0)
-
-    @pl.when(inner)
-    def _():
-        project(2, 1)
-
-    @pl.when(jnp.logical_not(inner))
-    def _():
-        @pl.when(home)
-        def _():
-            for part in range(PARTS):
-                for slot in (2, 3):
-                    relay(slot, part, False)
-
-        @pl.when(jnp.logical_not(home))
-        def _():
-            for part in range(PARTS):
-                for slot in (2, 3):
-                    tokens_here(slot, part)
-
-        normalize_slot(2)
-        normalize_slot(3)
-        for t in range(3):
-            project(t, 1)
+    project(2, 1)
 
     for z in range(4):
 
@@ -592,12 +595,13 @@
         def _():
             send_grads(h, 0).start()
 
-        from_x(3 + h)
         if h == 0:
-            start_own(5)
-        if h > 0:
-            from_y(2 + h)
-    from_y(5)
+            from_x(7)
+        if h == 1:
+            from_y(6)
+            from_x(8)
+    from_y(7)
+    from_y(8)
     for j in range(3, 6):
         weight_ready(j)
 
@@ -627,11 +631,12 @@
     grad_norm = out_ref[0] + back(core)
     out_ref[0] = norm_backward(grad_norm, normed_buf[...], inverse_buf[...], gain_ref[...][None])
 
+    for c in range(len(CHUNKS)):
+        x_copy(c, w).wait_send()
+        y_copy(c, g).wait_send()
+        passed_copy(c, across).wait_send()
     for j in range(6):
-        x_copy(j, w).wait_send()
         own_copy(j, w).wait_send()
-        y_copy(j, g).wait_send()
-        passed_copy(j, across).wait_send()
     for part in range(PARTS):
         send_tokens(part).wait_send()
 
@@ -703,8 +708,8 @@
             pltpu.VMEM((3, 4, 3, HEAD_DIM, ROWS), BF16),
             pltpu.VMEM((3, HD, ROWS), BF16),
             pltpu.SemaphoreType.DMA((10,)),
-            pltpu.SemaphoreType.DMA((4, 6)),
-            pltpu.SemaphoreType.DMA((4, 6)),
+            pltpu.SemaphoreType.DMA((4, len(CHUNKS))),
+            pltpu.SemaphoreType.DMA((4, len(CHUNKS))),
             pltpu.SemaphoreType.DMA((3, PARTS)),
             pltpu.SemaphoreType.DMA((4, PARTS)),
             pltpu.SemaphoreType.DMA((4, PARTS)),

time: 50.3 us -> 45.9 us (0.913)
  Pallas kernels: 48 us -> 43.5 us
    pallas_call x1, Pallas kernels: 48 us -> 43.5 us  [fused(): pl.pallas_call(fused_kernel, out_shape=jax.ShapeDtypeStruct((1, ROWS, WID...]
where the time goes in v2:
time: 45.9 us; the launch traced here: 45.6 us
  Pallas kernels  43.5 us (95%)
  local copies, waits for them, and re-layouts  2.07 us (5%)
    pallas_call x1, Pallas kernels, fused(): pl.pallas_call(fused_kernel, out_shape=jax.ShapeDtypeStruct((1, ROWS, WID...  43.5 us
    unnamed x1, local copies, waits for them, and re-layouts  2.07 us

profile of v2, /device:TPU:1, one launch (start us, length us, event | category | flops | bytes accessed | tf_op | source)
XLA Modules:
  0.0 45.6 jit_solution(13180619961380439231)
XLA Ops:
  0.0 43.5 %shard_map.100 = f32[1,128,1536]{2,1,0:T(8,128)} custom-call(bf16[1,128,1536]{2,1,0:T(8,128)(2,1)} %tokens_hbm.1, bf16[1,128,1536]{2,1,0:T(8,128)(2,1)} %upstream_hbm.1, f32[1536]{0:T(1024)} %gain_hbm.1, f32[1536]{0:T(1024)} %norm_bias_hbm.1, bf16[384,2304]{1,0:T(8,128)(2,1)} %codes_hbm.1, f32[3,18]{1,0:T(4,128)} %in_scales_hbm.1, f32[2304]{0:T(1024)} %in_bias_hbm.1, ...), custom_call_target="tpu_custom_call" | custom-call | flops 2500000000 | bytes 8000000 | tf_op jit(solution)/shard_map/pallas_call | solution.py:682
  43.6 2.1 %copy.12 = f32[1,128,1536]{2,1,0:T(8,128)} copy(f32[1,128,1536]{2,1,0:T(8,128)} %shard_map.100) | data formatting | bytes 1572864

commit v3 on v2

--- a/solution.py
+++ b/solution.py
@@ -167,9 +167,9 @@
 ROWS = 128
 SHARD = 384
 HALF = 384
-GROUP = 192
-CHUNKS = ((0, 0, 192), (0, 192, 192), (1, 0, 192), (1, 192, 192), (2, 0, 192), (2, 192, 192))
-CHUNKS += ((3, 0, 384), (4, 0, 384), (5, 0, 384))
+CHUNKS = tuple((p, 192 * r) for p in range(6) for r in range(2))
+CHUNK = 192
+BLOCK = 128
 PARTS = 4
 PART = ROWS // PARTS
 BF16 = jnp.bfloat16
@@ -235,12 +235,12 @@
     sibling = w + 1 - 2 * core
     far_sibling = lax.rem(sibling + 2, 4)
     side = s // 2
-    half = lax.rem(s, 2)
     home = core == side
     inner = lax.rem(s + side, 2) == 1
+    outer = jnp.logical_not(inner)
+    away = jnp.logical_not(home)
     owner = w - core + side
-    place = 2 * half + core
-    blocks = (s, s + 1 - 2 * half, 2 - side, 3 - 3 * side)
+    blocks = (s, s + 1 - 2 * lax.rem(s, 2), 2 - side, 3 - 3 * side)
 
     def load(index, source, target):
         copy = pltpu.make_async_copy(source, target, load_sem.at[index])
@@ -276,49 +276,46 @@
             device_id_type=MESH,
         )
 
-    def half_of(j):
-        return half if j < 3 else 1 - half
-
-    def columns_of(j):
-        return pl.ds(pl.multiple_of(768 * (j % 3) + HALF * half_of(j), 128), HALF)
-
-    def dequantize_chunk(j):
-        first = 6 * (j % 3) + 3 * half_of(j)
-        for rb in range(3):
-            for cb in range(3):
-                cols = pl.ds(pl.multiple_of(128 * (first + cb), 128), 128)
+    def block_at(p):
+        return jnp.where(inner, p, lax.rem(p + 4, 6))
+
+    def lanes(first):
+        return pl.ds(pl.multiple_of(first, BLOCK), BLOCK)
+
+    def dequantize_block(p):
+        b = block_at(p)
+        for t in range(3):
+            for rb in range(3):
                 rows = pl.ds(pl.multiple_of(SHARD * w + 128 * rb, 128), 128)
-                block = codes[128 * rb : 128 * (rb + 1), cols].astype(F32)
-                weight[rows, cols] = (block * in_scales[rb, first + cb]).astype(BF16)
-
-    def weight_copy(kind, index, j, row, count, peer):
-        part = weight.at[pl.ds(pl.multiple_of(row, 32), count), columns_of(j)]
+                block = codes[128 * rb : 128 * (rb + 1), lanes(HD * t + BLOCK * b)].astype(F32)
+                weight[t, rows, lanes(BLOCK * b)] = (block * in_scales[rb, 6 * t + b]).astype(BF16)
+
+    def weight_copy(kind, index, p, row, count, peer):
+        rows = pl.ds(pl.multiple_of(row, 32), count)
+        part = weight.at[:, rows, lanes(BLOCK * block_at(p))]
         return remote(part, part, w_send.at[kind, index], w_recv.at[kind, index], peer)
 
     def x_copy(c, shard):
-        j, first, count = CHUNKS[c]
-        row = SHARD * shard + first + count // 2 * g
-        return weight_copy(0, c, j, row, count // 2, {"weight": across})
+        p, first = CHUNKS[c]
+        row = SHARD * shard + first + CHUNK // 2 * g
+        return weight_copy(0, c, p, row, CHUNK // 2, {"weight": across})
 
     def y_copy(c, part):
-        j, first, count = CHUNKS[c]
-        row = SHARD * across + first + count // 2 * part
-        return weight_copy(1, c, j, row, count // 2, {"groups": 1 - g})
-
-    def own_copy(j, shard):
-        return weight_copy(2, j, j, SHARD * shard, SHARD, {"weight": sibling})
+        p, first = CHUNKS[c]
+        row = SHARD * across + first + CHUNK // 2 * part
+        return weight_copy(1, c, p, row, CHUNK // 2, {"groups": 1 - g})
+
+    def own_copy(p, shard):
+        return weight_copy(2, p, p, SHARD * shard, SHARD, {"weight": sibling})
 
     def passed_copy(c, shard):
-        j, first, count = CHUNKS[c]
-        return weight_copy(3, c, j, SHARD * shard + first, count, {"weight": sibling})
-
-    def chunks_of(j):
-        return [c for c in range(len(CHUNKS)) if CHUNKS[c][0] == j]
-
-    def start_own(j):
-        for c in chunks_of(j):
-            x_copy(c, w).start()
-        own_copy(j, w).start()
+        p, first = CHUNKS[c]
+        return weight_copy(3, c, p, SHARD * shard + first, CHUNK, {"weight": sibling})
+
+    def start_own(p):
+        for r in range(2):
+            x_copy(2 * p + r, w).start()
+        own_copy(p, w).start()
 
     def from_x(c):
         x_copy(c, across).wait_recv()
@@ -328,10 +325,11 @@
         y_copy(c, 1 - g).wait_recv()
         passed_copy(c, across).start()
 
-    def weight_ready(j):
-        own_copy(j, sibling).wait_recv()
-        for c in chunks_of(j):
-            passed_copy(c, far_sibling).wait_recv()
+    def weight_ready(p):
+        own_copy(p, sibling).wait_recv()
+        for r in range(2):
+            row = SHARD * far_sibling + CHUNK * r
+            weight_copy(3, 2 * p + r, p, row, CHUNK, {"weight": sibling}).wait_recv()
 
     def part_rows(part):
         return pl.ds(PART * part, PART)
@@ -368,27 +366,24 @@
             forward_tokens(slot, part).start()
         pass_tokens(slot, part).start()
 
-    def share(q):
-        peer = {"seq": 2 * core + q // 2, "weight": w - core + q % 2}
+    def share(d):
+        count = 256 if d < 2 else 128
+        first = 256 * d if d < 2 else 256 + 128 * d
+        rows = packed.at[first : first + count, :]
+        peer = {"seq": 1 + core if d < 2 else 3 * core, "weight": w - core + d % 2}
+        return remote(rows, gathered.at[s, 0:count, :], a_send.at[d], a_recv.at[s], peer)
+
+    def share_done(z, count):
         return remote(
-            packed.at[GROUP * q : GROUP * (q + 1), :],
-            gathered.at[s],
-            a_send.at[q],
-            a_recv.at[s],
-            peer,
-        )
-
-    def share_done(z):
-        return remote(
-            packed.at[0:GROUP, :],
-            gathered.at[z],
+            packed.at[0:count, :],
+            gathered.at[z, 0:count, :],
             a_send.at[0],
             a_recv.at[z],
             {"weight": sibling},
         )
 
-    def stays(q):
-        return home & (place == q)
+    def stays(d):
+        return home & (inner if d < 2 else outer) & (core == d % 2)
 
     def head_gradients(part):
         for rb in range(3):
@@ -400,40 +395,50 @@
                     block * out_scales[3 * part + rb, cb]
                 ).astype(BF16)
         value = lax.dot_general(out_weight[...], scaled[...], NT, preferred_element_type=F32)
-        packed[HALF * part : HALF * (part + 1), :] = value.astype(BF16)
-        for q in (2 * part, 2 * part + 1):
-
-            @pl.when(jnp.logical_not(stays(q)))
+        value = value.astype(BF16)
+        for rb in range(3):
+            place = (0, 2, 1, 3, 4, 5)[3 * part + rb]
+            packed[BLOCK * place : BLOCK * (place + 1), :] = value[128 * rb : 128 * (rb + 1), :]
+
+    def share_all():
+        for d in range(4):
+            count = 256 if d < 2 else 128
+            first = 256 * d if d < 2 else 256 + 128 * d
+
+            @pl.when(jnp.logical_not(stays(d)))
             def _():
-                share(q).start()
-
-            @pl.when(stays(q))
+                share(d).start()
+
+            @pl.when(stays(d))
             def _():
-                gathered[s] = packed[GROUP * q : GROUP * (q + 1), :]
+                gathered[s, 0:count, :] = packed[first : first + count, :]
 
     def normalize_slot(slot):
         norm_out[ROWS * slot : ROWS * (slot + 1), :] = normalize(
             raw[blocks[slot]].astype(F32), gain_ref[...][None], norm_bias_ref[...][None]
         )[2]
 
-    def project(t, pair):
-        first = pl.multiple_of(768 * t + HALF * half + 128 * core, 128)
-        value = jnp.dot(
-            norm_out[256 * pair : 256 * (pair + 1), :],
-            weight[:, pl.ds(first, 256)],
-            preferred_element_type=F32,
-        )
-        value = value + in_bias_ref[pl.ds(first, 256)][None]
-        if t == 0:
-            value = value * HEAD_DIM ** (-0.5)
-        projected[t, :, 256 * pair : 256 * (pair + 1)] = value.T.astype(BF16)
+    def project(n, first, count):
+        b = block_at(2 * n + core)
+        columns = jnp.concatenate([weight[t, :, lanes(BLOCK * b)] for t in range(3)], axis=1)
+        value = jnp.dot(norm_out[first : first + count, :], columns, preferred_element_type=F32)
+        for t in range(3):
+            part = value[:, BLOCK * t : BLOCK * (t + 1)]
+            part = part + in_bias_ref[lanes(HD * t + BLOCK * b)][None]
+            if t == 0:
+                part = part * HEAD_DIM ** (-0.5)
+            projected[n, t, :, first : first + count] = part.T.astype(BF16)
+
+    pl.semaphore_wait(barrier, len(peers))
+
+    @pl.when(inner | home)
+    def _():
+        for part in range(PARTS):
+            send_tokens(part).start()
 
     load_in_scales.wait()
     load_codes.wait()
-    dequantize_chunk(0)
-    pl.semaphore_wait(barrier, len(peers))
-    for part in range(PARTS):
-        send_tokens(part).start()
+    dequantize_block(0)
     start_own(0)
 
     @pl.when(home)
@@ -441,9 +446,9 @@
         for part in range(PARTS):
             pass_tokens(0, part).start()
 
-    for j in range(1, 6):
-        dequantize_chunk(j)
-        start_own(j)
+    for p in range(1, 6):
+        dequantize_block(p)
+        start_own(p)
 
     load_layer_scale.wait()
     load_upstream.wait()
@@ -452,6 +457,13 @@
     load_out_codes.wait()
     head_gradients(0)
     head_gradients(1)
+
+    @pl.when(outer & away)
+    def _():
+        for part in range(PARTS):
+            send_tokens(part).start()
+
+    share_all()
 
     load_gain.wait()
     load_norm_bias.wait()
@@ -467,107 +479,101 @@
     def _():
         norm_out[0:ROWS, :] = rounded
 
-    def relay_inner(part):
+    def relay_inner(slot, *parts):
         @pl.when(home & inner)
         def _():
-            relay(2, part, True)
-            relay(3, part, True)
-
-        @pl.when(home)
-        def _():
-            relay(1, part, False)
-
-    def relay_outer(part):
-        @pl.when(home & jnp.logical_not(inner))
-        def _():
-            relay(2, part, False)
-            relay(3, part, False)
-
-    def await_tokens(slots):
-        @pl.when(jnp.logical_not(home))
-        def _():
-            for part in range(PARTS):
-                for slot in slots:
+            for part in parts:
+                relay(slot, part, slot > 1)
+
+    def relay_outer(slot, *parts):
+        @pl.when(home & outer)
+        def _():
+            for part in parts:
+                relay(slot, part, False)
+
+    def await_tokens(*slots):
+        @pl.when(away)
+        def _():
+            for slot in slots:
+                for part in range(PARTS):
                     tokens_here(slot, part)
 
+    relay_inner(2, 0, 1)
     from_x(0)
-    relay_inner(0)
+    relay_outer(1, 0, 1)
+    relay_inner(2, 2)
+    relay_inner(1, 0, 1)
     from_x(1)
-    relay_inner(1)
+    relay_outer(1, 2, 3)
     from_x(2)
+    relay_inner(2, 3)
+    relay_inner(3, 0)
     from_y(0)
-    relay_outer(0)
-    relay_inner(2)
+    relay_inner(3, 1)
+    relay_outer(2, 0)
     from_x(3)
     from_y(1)
-    relay_outer(1)
+    relay_inner(1, 2, 3)
+    relay_outer(2, 1)
+    relay_inner(3, 2)
     from_x(4)
-    relay_inner(3)
     from_y(2)
-    await_tokens((0, 1))
-
-    @pl.when(jnp.logical_not(home))
+    relay_outer(2, 2, 3)
+    relay_inner(3, 3)
+    await_tokens(0, 1)
+
+    @pl.when(away)
     def _():
         normalize_slot(0)
 
     normalize_slot(1)
     from_x(5)
     from_y(3)
-    relay_outer(2)
-    weight_ready(0)
-    project(0, 0)
-
-    @pl.when(inner)
-    def _():
-        await_tokens((2, 3))
-        normalize_slot(2)
-        normalize_slot(3)
-        project(0, 1)
-
+    relay_outer(3, 0)
+    await_tokens(2)
+    normalize_slot(2)
+    from_x(6)
     from_y(4)
-    relay_outer(3)
-    weight_ready(1)
-    project(1, 0)
+    relay_outer(3, 1)
+    weight_ready(core)
+    project(0, 0, 3 * ROWS)
+    from_x(7)
     from_y(5)
-
-    @pl.when(jnp.logical_not(inner))
-    def _():
-        await_tokens((2, 3))
-        normalize_slot(2)
-        normalize_slot(3)
-        project(0, 1)
-
-    project(1, 1)
-    from_x(6)
-    weight_ready(2)
-    project(2, 0)
-    project(2, 1)
+    relay_outer(3, 2, 3)
+    await_tokens(3)
+    normalize_slot(3)
+    project(0, 3 * ROWS, ROWS)
 
     for z in range(4):
 
-        @pl.when(jnp.logical_not(home & (s == z)))
-        def _():
-            share_done(z).wait_recv()
-
-    def grad_copy(h, slot, q, peer):
-        rows = pl.ds(pl.multiple_of(GROUP * q + HEAD_DIM * h, 64), HEAD_DIM)
+        @pl.when(jnp.logical_not(home & (s == z)) & inner)
+        def _():
+            share_done(z, 256).wait_recv()
+
+        @pl.when(jnp.logical_not(home & (s == z)) & outer)
+        def _():
+            share_done(z, 128).wait_recv()
+
+    def grad_copy(h, slot, b, peer):
+        rows = pl.ds(pl.multiple_of(BLOCK * b + HEAD_DIM * (h % 2), 64), HEAD_DIM)
         return remote(
             grads.at[h, slot],
             grad_proj.at[:, rows, :],
             g_send.at[h, slot],
-            g_recv.at[h, q],
+            g_recv.at[2 * b + h % 2],
             peer,
         )
 
     def send_grads(h, slot):
-        return grad_copy(h, slot, place, {"seq": blocks[slot], "weight": owner})
-
-    for h in range(3):
-        mine = pl.ds(pl.multiple_of(HEAD_DIM * core + HEAD_DIM * h, 64), HEAD_DIM)
-        q_t, k_t, v_t = (projected[t, mine, :] for t in range(3))
-        g_t = jnp.concatenate(
-            [gathered[z, HEAD_DIM * h : HEAD_DIM * (h + 1), :] for z in blocks], axis=1
-        )
+        b = block_at(h // 2 * 2 + core)
+        return grad_copy(h, slot, b, {"seq": blocks[slot], "weight": owner})
+
+    def attend(h):
+        n, i = h // 2, h % 2
+        rows = slice(HEAD_DIM * i, HEAD_DIM * (i + 1))
+        q_t, k_t, v_t = (projected[n, t, rows, :] for t in range(3))
+        g_rows = slice(HEAD_DIM * h, HEAD_DIM * (h + 1))
+        g_t = jnp.concatenate([gathered[z, g_rows, :] for z in blocks], axis=1)
         scores = jnp.dot(k_t.T, q_t, preferred_element_type=F32)
         dprob = jnp.dot(v_t.T, g_t, preferred_element_type=F32)
         expo = jnp.exp(scores - jnp.max(scores, axis=0, keepdims=True))
@@ -581,62 +587,83 @@
         )
         for t in range(3):
             value = parts[t].astype(BF16)
-            for i in range(4):
-                grads[h, i, t] = value[:, ROWS * i : ROWS * (i + 1)]
+            for slot in range(4):
+                grads[h, slot, t] = value[:, ROWS * slot : ROWS * (slot + 1)]
         for slot in (3, 2, 1):
             send_grads(h, slot).start()
 
         @pl.when(home)
         def _():
-            own = pl.ds(pl.multiple_of(GROUP * place + HEAD_DIM * h, 64), HEAD_DIM)
+            first = BLOCK * block_at(2 * n + core) + HEAD_DIM * i
+            own = pl.ds(pl.multiple_of(first, 64), HEAD_DIM)
             grad_proj[:, own, :] = grads[h, 0]
 
-        @pl.when(jnp.logical_not(home))
+        @pl.when(away)
         def _():
             send_grads(h, 0).start()
 
-        if h == 0:
-            from_x(7)
-        if h == 1:
-            from_y(6)
-            from_x(8)
+    attend(0)
+    from_x(8)
+    from_y(6)
+    attend(1)
+    from_x(9)
     from_y(7)
+    from_x(10)
     from_y(8)
-    for j in range(3, 6):
-        weight_ready(j)
-
-    def grads_ready(part):
-        for h in range(3):
-            for k in range(2):
-                q = 2 * part + k
-
-                @pl.when(jnp.logical_not(home & (place == q)))
+
+    @pl.when(inner)
+    def _():
+        weight_ready(2 + core)
+        project(1, 0, 4 * ROWS)
+        attend(2)
+        from_x(11)
+        from_y(9)
+        attend(3)
+
+    @pl.when(outer)
+    def _():
+        from_x(11)
+        from_y(9)
+        weight_ready(2 + core)
+
+    from_y(10)
+    from_y(11)
+    weight_ready(1 - core)
+    weight_ready(3 - core)
+    weight_ready(4)
+    weight_ready(5)
+
+    def grads_ready(first, count):
+        for b in range(first, first + count):
+            mine = home & (inner if b < 4 else outer) & (core == b % 2)
+            for i in range(2):
+
+                @pl.when(jnp.logical_not(mine))
                 def _():
-                    grad_copy(h, 0, q, {"weight": sibling}).wait_recv()
-
-    def back(part):
+                    grad_copy(i, 0, b, {"weight": sibling}).wait_recv()
+
+    def back(first, count):
         total = None
+        part = slice(BLOCK * first, BLOCK * (first + count))
         for t in range(3):
-            rows = pl.ds(pl.multiple_of(HALF * part, 128), HALF)
-            cols = pl.ds(pl.multiple_of(768 * t + HALF * part, 128), HALF)
             term = lax.dot_general(
-                grad_proj[t, rows, :].T, weight[:, cols], NT, preferred_element_type=F32
+                grad_proj[t, part, :].T, weight[t, :, part], NT, preferred_element_type=F32
             )
             total = term if total is None else total + term
         return total
 
-    grads_ready(1 - core)
-    out_ref[0] = back(1 - core)
-    grads_ready(core)
-    grad_norm = out_ref[0] + back(core)
+    grads_ready(0, 4)
+    out_ref[0] = back(0, 4)
+    grads_ready(4, 2)
+    grad_norm = out_ref[0] + back(4, 2)
     out_ref[0] = norm_backward(grad_norm, normed_buf[...], inverse_buf[...], gain_ref[...][None])
 
     for c in range(len(CHUNKS)):
         x_copy(c, w).wait_send()
         y_copy(c, g).wait_send()
         passed_copy(c, across).wait_send()
-    for j in range(6):
-        own_copy(j, w).wait_send()
+    for p in range(6):
+        own_copy(p, w).wait_send()
     for part in range(PARTS):
         send_tokens(part).wait_send()
 
@@ -650,19 +677,26 @@
             for slot in (2, 3):
                 forward_tokens(slot, part).wait_send()
 
-    for q in range(4):
-
-        @pl.when(jnp.logical_not(stays(q)))
-        def _():
-            share(q).wait_send()
-
-    for h in range(3):
-        for slot in (1, 2, 3):
-            send_grads(h, slot).wait_send()
-
-        @pl.when(jnp.logical_not(home))
-        def _():
-            send_grads(h, 0).wait_send()
+    for d in range(4):
+
+        @pl.when(jnp.logical_not(stays(d)))
+        def _():
+            share(d).wait_send()
+
+    def grads_sent(heads):
+        for h in heads:
+            for slot in (1, 2, 3):
+                send_grads(h, slot).wait_send()
+
+            @pl.when(away)
+            def _():
+                send_grads(h, 0).wait_send()
+
+    grads_sent((0, 1))
+
+    @pl.when(inner)
+    def _():
+        grads_sent((2, 3))
 
 
 def fused(
@@ -691,7 +725,7 @@
             pltpu.VMEM((3 * HD,), F32),
             pltpu.SMEM((6, 12), F32),
             pltpu.VMEM((WIDTH,), F32),
-            pltpu.VMEM((WIDTH, 3 * HD), BF16),
+            pltpu.VMEM((3, WIDTH, HD), BF16),
             pltpu.VMEM((SHARD, 3 * HD), BF16),
             pltpu.VMEM((HD, WIDTH), BF16),
             pltpu.VMEM((HALF, WIDTH), BF16),
@@ -703,9 +737,9 @@
             pltpu.VMEM((4 * ROWS, WIDTH), BF16),
             pltpu.VMEM((ROWS, WIDTH), BF16),
             pltpu.VMEM((HD, ROWS), BF16),
-            pltpu.VMEM((4, GROUP, ROWS), BF16),
-            pltpu.VMEM((3, 256, 4 * ROWS), BF16),
-            pltpu.VMEM((3, 4, 3, HEAD_DIM, ROWS), BF16),
+            pltpu.VMEM((4, 2 * BLOCK, ROWS), BF16),
+            pltpu.VMEM((2, 3, BLOCK, 4 * ROWS), BF16),
+            pltpu.VMEM((4, 4, 3, HEAD_DIM, ROWS), BF16),
             pltpu.VMEM((3, HD, ROWS), BF16),
             pltpu.SemaphoreType.DMA((10,)),
             pltpu.SemaphoreType.DMA((4, len(CHUNKS))),
@@ -715,8 +749,8 @@
             pltpu.SemaphoreType.DMA((4, PARTS)),
             pltpu.SemaphoreType.DMA((4,)),
             pltpu.SemaphoreType.DMA((4,)),
-            pltpu.SemaphoreType.DMA((3, 4)),
-            pltpu.SemaphoreType.DMA((3, 4)),
+            pltpu.SemaphoreType.DMA((4, 4)),
+            pltpu.SemaphoreType.DMA((12,)),
         ],
         compiler_params=pltpu.CompilerParams(
             collective_id=0, has_side_effects=True, vmem_limit_bytes=64 * 1024 * 1024 - 65536

time: 45.9 us -> 44.4 us (0.967)
  Pallas kernels: 43.5 us -> 42.2 us
    pallas_call x1, Pallas kernels: 43.5 us -> 42.2 us  [fused(): pl.pallas_call(fused_kernel, out_shape=jax.ShapeDtypeStruct((1, ROWS, WID...]
where the time goes in v3:
time: 44.4 us; the launch traced here: 44.3 us
  Pallas kernels  42.2 us (95%)
  local copies, waits for them, and re-layouts  2.07 us (5%)
    pallas_call x1, Pallas kernels, fused(): pl.pallas_call(fused_kernel, out_shape=jax.ShapeDtypeStruct((1, ROWS, WID...  42.2 us
    unnamed x1, local copies, waits for them, and re-layouts  2.07 us

profile of v3, /device:TPU:1, one launch (start us, length us, event | category | flops | bytes accessed | tf_op | source)
XLA Modules:
  0.0 44.3 jit_solution(2690820567520361485)
XLA Ops:
  0.0 42.2 %shard_map.100 = f32[1,128,1536]{2,1,0:T(8,128)} custom-call(bf16[1,128,1536]{2,1,0:T(8,128)(2,1)} %tokens_hbm.1, bf16[1,128,1536]{2,1,0:T(8,128)(2,1)} %upstream_hbm.1, f32[1536]{0:T(1024)} %gain_hbm.1, f32[1536]{0:T(1024)} %norm_bias_hbm.1, bf16[384,2304]{1,0:T(8,128)(2,1)} %codes_hbm.1, f32[3,18]{1,0:T(4,128)} %in_scales_hbm.1, f32[2304]{0:T(1024)} %in_bias_hbm.1, ...), custom_call_target="tpu_custom_call" | custom-call | flops 2500000000 | bytes 8000000 | tf_op jit(solution)/shard_map/pallas_call | solution.py:716
  42.2 2.1 %copy.12 = f32[1,128,1536]{2,1,0:T(8,128)} copy(f32[1,128,1536]{2,1,0:T(8,128)} %shard_map.100) | data formatting | bytes 1572864

commit v4 on v3

--- a/solution.py
+++ b/solution.py
@@ -201,6 +201,7 @@
     out_scales,
     layer_scale_ref,
     weight,
+    first_codes,
     codes,
     out_codes,
     out_weight,
@@ -242,12 +243,22 @@
     owner = w - core + side
     blocks = (s, s + 1 - 2 * lax.rem(s, 2), 2 - side, 3 - 3 * side)
 
+    def block_at(p):
+        return jnp.where(inner, p, lax.rem(p + 4, 6))
+
+    def lanes(first):
+        return pl.ds(pl.multiple_of(first, BLOCK), BLOCK)
+
     def load(index, source, target):
         copy = pltpu.make_async_copy(source, target, load_sem.at[index])
         copy.start()
         return copy
 
     load_in_scales = load(4, in_scales_hbm, in_scales)
+    load_first = [
+        load(10 + t, codes_hbm.at[:, lanes(HD * t + BLOCK * block_at(0))], first_codes.at[t])
+        for t in range(3)
+    ]
     load_codes = load(0, codes_hbm, codes)
     load_upstream = load(2, upstream_hbm.at[0], upstream)
     load_out_codes = load(3, out_codes_hbm, out_codes)
@@ -276,18 +287,16 @@
             device_id_type=MESH,
         )
 
-    def block_at(p):
-        return jnp.where(inner, p, lax.rem(p + 4, 6))
-
-    def lanes(first):
-        return pl.ds(pl.multiple_of(first, BLOCK), BLOCK)
-
     def dequantize_block(p):
         b = block_at(p)
         for t in range(3):
             for rb in range(3):
                 rows = pl.ds(pl.multiple_of(SHARD * w + 128 * rb, 128), 128)
-                block = codes[128 * rb : 128 * (rb + 1), lanes(HD * t + BLOCK * b)].astype(F32)
+                if p == 0:
+                    block = first_codes[t, 128 * rb : 128 * (rb + 1), :]
+                else:
+                    block = codes[128 * rb : 128 * (rb + 1), lanes(HD * t + BLOCK * b)]
+                block = block.astype(F32)
                 weight[t, rows, lanes(BLOCK * b)] = (block * in_scales[rb, 6 * t + b]).astype(BF16)
 
     def weight_copy(kind, index, p, row, count, peer):
@@ -429,6 +438,10 @@
                 part = part * HEAD_DIM ** (-0.5)
             projected[n, t, :, first : first + count] = part.T.astype(BF16)
 
+    load_in_scales.wait()
+    for copy in load_first:
+        copy.wait()
+    dequantize_block(0)
     pl.semaphore_wait(barrier, len(peers))
 
     @pl.when(inner | home)
@@ -436,9 +449,6 @@
         for part in range(PARTS):
             send_tokens(part).start()
 
-    load_in_scales.wait()
-    load_codes.wait()
-    dequantize_block(0)
     start_own(0)
 
     @pl.when(home)
@@ -446,6 +456,7 @@
         for part in range(PARTS):
             pass_tokens(0, part).start()
 
+    load_codes.wait()
     for p in range(1, 6):
         dequantize_block(p)
         start_own(p)
@@ -517,42 +528,25 @@
     relay_outer(2, 1)
     relay_inner(3, 2)
     from_x(4)
+    relay_outer(2, 2)
+    relay_inner(3, 3)
     from_y(2)
-    relay_outer(2, 2, 3)
-    relay_inner(3, 3)
-    await_tokens(0, 1)
-
+    relay_outer(2, 3)
     @pl.when(away)
     def _():
+        for slot in (0, 1):
+            for part in range(PARTS):
+                tokens_here(slot, part)
         normalize_slot(0)
 
     normalize_slot(1)
-    from_x(5)
-    from_y(3)
-    relay_outer(3, 0)
-    await_tokens(2)
-    normalize_slot(2)
-    from_x(6)
-    from_y(4)
-    relay_outer(3, 1)
-    weight_ready(core)
-    project(0, 0, 3 * ROWS)
-    from_x(7)
-    from_y(5)
-    relay_outer(3, 2, 3)
-    await_tokens(3)
-    normalize_slot(3)
-    project(0, 3 * ROWS, ROWS)
-
-    for z in range(4):
-
-        @pl.when(jnp.logical_not(home & (s == z)) & inner)
-        def _():
-            share_done(z, 256).wait_recv()
-
-        @pl.when(jnp.logical_not(home & (s == z)) & outer)
-        def _():
-            share_done(z, 128).wait_recv()
+
+    def shared(count):
+        for z in range(4):
+
+            @pl.when(jnp.logical_not(home & (s == z)))
+            def _():
+                share_done(z, count).wait_recv()
 
     def grad_copy(h, slot, b, peer):
         rows = pl.ds(pl.multiple_of(BLOCK * b + HEAD_DIM * (h % 2), 64), HEAD_DIM)
@@ -602,36 +596,84 @@
         def _():
             send_grads(h, 0).start()
 
-    attend(0)
-    from_x(8)
-    from_y(6)
-    attend(1)
-    from_x(9)
-    from_y(7)
-    from_x(10)
-    from_y(8)
-
     @pl.when(inner)
     def _():
-        weight_ready(2 + core)
-        project(1, 0, 4 * ROWS)
+        await_tokens(2, 3)
+        normalize_slot(2)
+        normalize_slot(3)
+        from_x(5)
+        from_y(3)
+        from_x(6)
+        weight_ready(core)
+        project(0, 0, 4 * ROWS)
+        shared(256)
+
+        @pl.when(core == 1)
+        def _():
+            from_x(7)
+
+        attend(0)
+
+        @pl.when(core == 0)
+        def _():
+            from_x(7)
+
+        from_y(4)
+        attend(1)
+        from_x(8)
+        from_y(5)
+        from_x(9)
+        from_y(6)
+
+        @pl.when(core == 0)
+        def _():
+            weight_ready(2)
+            project(1, 0, 4 * ROWS)
+
+        from_x(10)
+        from_y(7)
+
+        @pl.when(core == 1)
+        def _():
+            weight_ready(3)
+            project(1, 0, 4 * ROWS)
+
         attend(2)
         from_x(11)
-        from_y(9)
+        from_y(8)
         attend(3)
 
     @pl.when(outer)
     def _():
+        from_x(5)
+        relay_outer(3, 0)
+        await_tokens(2)
+        normalize_slot(2)
+        from_y(3)
+        from_x(6)
+        relay_outer(3, 1)
+        weight_ready(core)
+        project(0, 0, 3 * ROWS)
+        from_x(7)
+        from_y(4)
+        relay_outer(3, 2)
+        from_x(8)
+        from_y(5)
+        relay_outer(3, 3)
+        await_tokens(3)
+        normalize_slot(3)
+        project(0, 3 * ROWS, ROWS)
+        shared(128)
+        from_x(9)
+        attend(0)
+        from_x(10)
+        from_y(6)
+        attend(1)
         from_x(11)
-        from_y(9)
-        weight_ready(2 + core)
-
-    from_y(10)
-    from_y(11)
-    weight_ready(1 - core)
-    weight_ready(3 - core)
-    weight_ready(4)
-    weight_ready(5)
+        from_y(7)
+        from_y(8)
+
+    from_y(9)
 
     def grads_ready(first, count):
         for b in range(first, first + count):
@@ -652,10 +694,45 @@
             total = term if total is None else total + term
         return total
 
-    grads_ready(0, 4)
-    out_ref[0] = back(0, 4)
+    @pl.when(inner)
+    def _():
+        weight_ready(1 - core)
+
+    @pl.when(outer)
+    def _():
+        weight_ready(2)
+        weight_ready(3)
+
+    from_y(10)
+    from_y(11)
+    grads_ready(0, 2)
+    out_ref[0] = back(0, 2)
+
+    @pl.when(inner)
+    def _():
+        weight_ready(4)
+        weight_ready(5)
+
+    @pl.when(outer)
+    def _():
+        weight_ready(1 - core)
+
     grads_ready(4, 2)
-    grad_norm = out_ref[0] + back(4, 2)
+    out_ref[0] += back(4, 2)
+
+    @pl.when(inner)
+    def _():
+        weight_ready(3 - core)
+
+    @pl.when(outer)
+    def _():
+        weight_ready(4)
+        weight_ready(5)
+
+    grads_ready(2, 1)
+    out_ref[0] += back(2, 1)
+    grads_ready(3, 1)
+    grad_norm = out_ref[0] + back(3, 1)
     out_ref[0] = norm_backward(grad_norm, normed_buf[...], inverse_buf[...], gain_ref[...][None])
 
     for c in range(len(CHUNKS)):
@@ -726,6 +803,7 @@
             pltpu.SMEM((6, 12), F32),
             pltpu.VMEM((WIDTH,), F32),
             pltpu.VMEM((3, WIDTH, HD), BF16),
+            pltpu.VMEM((3, SHARD, BLOCK), BF16),
             pltpu.VMEM((SHARD, 3 * HD), BF16),
             pltpu.VMEM((HD, WIDTH), BF16),
             pltpu.VMEM((HALF, WIDTH), BF16),
@@ -741,7 +819,7 @@
             pltpu.VMEM((2, 3, BLOCK, 4 * ROWS), BF16),
             pltpu.VMEM((4, 4, 3, HEAD_DIM, ROWS), BF16),
             pltpu.VMEM((3, HD, ROWS), BF16),
-            pltpu.SemaphoreType.DMA((10,)),
+            pltpu.SemaphoreType.DMA((13,)),
             pltpu.SemaphoreType.DMA((4, len(CHUNKS))),
             pltpu.SemaphoreType.DMA((4, len(CHUNKS))),
             pltpu.SemaphoreType.DMA((3, PARTS)),

time: 44.4 us -> 41.5 us (0.935)
  Pallas kernels: 42.2 us -> 39.2 us
    pallas_call x1, Pallas kernels: 42.2 us -> 39.2 us  [fused(): pl.pallas_call(fused_kernel, out_shape=jax.ShapeDtypeStruct((1, ROWS, WID...]
where the time goes in v4:
time: 41.5 us; the launch traced here: 41.3 us
  Pallas kernels  39.2 us (94%)
  local copies, waits for them, and re-layouts  2.07 us (5%)
    pallas_call x1, Pallas kernels, fused(): pl.pallas_call(fused_kernel, out_shape=jax.ShapeDtypeStruct((1, ROWS, WID...  39.2 us
    unnamed x1, local copies, waits for them, and re-layouts  2.07 us

profile of v4, /device:TPU:1, one launch (start us, length us, event | category | flops | bytes accessed | tf_op | source)
XLA Modules:
  0.0 41.3 jit_solution(941183343392985745)
XLA Ops:
  0.0 39.2 %shard_map.100 = f32[1,128,1536]{2,1,0:T(8,128)} custom-call(bf16[1,128,1536]{2,1,0:T(8,128)(2,1)} %tokens_hbm.1, bf16[1,128,1536]{2,1,0:T(8,128)(2,1)} %upstream_hbm.1, f32[1536]{0:T(1024)} %gain_hbm.1, f32[1536]{0:T(1024)} %norm_bias_hbm.1, bf16[384,2304]{1,0:T(8,128)(2,1)} %codes_hbm.1, f32[3,18]{1,0:T(4,128)} %in_scales_hbm.1, f32[2304]{0:T(1024)} %in_bias_hbm.1, ...), custom_call_target="tpu_custom_call" | custom-call | flops 2500000000 | bytes 8000000 | tf_op jit(solution)/shard_map/pallas_call | solution.py:793
  39.2 2.1 %copy.12 = f32[1,128,1536]{2,1,0:T(8,128)} copy(f32[1,128,1536]{2,1,0:T(8,128)} %shard_map.100) | data formatting | bytes 1572864

commit v5 on v4

--- a/solution.py
+++ b/solution.py
@@ -214,6 +214,7 @@
     scaled,
     packed,
     gathered,
+    partial,
     projected,
     grads,
     grad_proj,
@@ -334,8 +335,12 @@
         y_copy(c, 1 - g).wait_recv()
         passed_copy(c, across).start()
 
-    def weight_ready(p):
+    def weight_near(p):
         own_copy(p, sibling).wait_recv()
+
+    def weight_ready(p, near=True):
+        if near:
+            weight_near(p)
         for r in range(2):
             row = SHARD * far_sibling + CHUNK * r
             weight_copy(3, 2 * p + r, p, row, CHUNK, {"weight": sibling}).wait_recv()
@@ -427,10 +432,19 @@
             raw[blocks[slot]].astype(F32), gain_ref[...][None], norm_bias_ref[...][None]
         )[2]
 
+    def product(n, first, count, chip):
+        b = block_at(2 * n + core)
+        span = pl.ds(pl.multiple_of(2 * SHARD * chip, 128), 2 * SHARD)
+        columns = jnp.concatenate([weight[t, span, lanes(BLOCK * b)] for t in range(3)], axis=1)
+        rows = norm_out[first : first + count, span]
+        return jnp.dot(rows, columns, preferred_element_type=F32)
+
+    def project_near(n, first, count):
+        partial[first : first + count, :] = product(n, first, count, w // 2)
+
     def project(n, first, count):
         b = block_at(2 * n + core)
-        columns = jnp.concatenate([weight[t, :, lanes(BLOCK * b)] for t in range(3)], axis=1)
-        value = jnp.dot(norm_out[first : first + count, :], columns, preferred_element_type=F32)
+        value = partial[first : first + count, :] + product(n, first, count, 1 - w // 2)
         for t in range(3):
             part = value[:, BLOCK * t : BLOCK * (t + 1)]
             part = part + in_bias_ref[lanes(HD * t + BLOCK * b)][None]
@@ -583,8 +597,10 @@
             value = parts[t].astype(BF16)
             for slot in range(4):
                 grads[h, slot, t] = value[:, ROWS * slot : ROWS * (slot + 1)]
-        for slot in (3, 2, 1):
+        for slot in (3, 1) if h == 2 else (3, 2, 1):
             send_grads(h, slot).start()
+        if h == 3:
+            send_grads(2, 2).start()
 
         @pl.when(home)
         def _():
@@ -602,42 +618,38 @@
         normalize_slot(2)
         normalize_slot(3)
         from_x(5)
+        weight_near(core)
+        project_near(0, 0, 4 * ROWS)
         from_y(3)
         from_x(6)
-        weight_ready(core)
+        weight_ready(core, False)
         project(0, 0, 4 * ROWS)
         shared(256)
 
+        from_x(7)
+        attend(0)
+        from_y(4)
+
         @pl.when(core == 1)
         def _():
-            from_x(7)
-
-        attend(0)
+            from_x(8)
+            from_y(5)
+
+        attend(1)
 
         @pl.when(core == 0)
         def _():
-            from_x(7)
-
-        from_y(4)
-        attend(1)
-        from_x(8)
-        from_y(5)
+            from_x(8)
+            from_y(5)
+
         from_x(9)
+        weight_near(2 + core)
+        project_near(1, 0, 4 * ROWS)
         from_y(6)
-
-        @pl.when(core == 0)
-        def _():
-            weight_ready(2)
-            project(1, 0, 4 * ROWS)
-
+        from_y(7)
+        weight_ready(2 + core, False)
+        project(1, 0, 4 * ROWS)
         from_x(10)
-        from_y(7)
-
-        @pl.when(core == 1)
-        def _():
-            weight_ready(3)
-            project(1, 0, 4 * ROWS)
-
         attend(2)
         from_x(11)
         from_y(8)
@@ -652,7 +664,9 @@
         from_y(3)
         from_x(6)
         relay_outer(3, 1)
-        weight_ready(core)
+        weight_near(core)
+        project_near(0, 0, 3 * ROWS)
+        weight_ready(core, False)
         project(0, 0, 3 * ROWS)
         from_x(7)
         from_y(4)
@@ -662,6 +676,7 @@
         relay_outer(3, 3)
         await_tokens(3)
         normalize_slot(3)
+        project_near(0, 3 * ROWS, ROWS)
         project(0, 3 * ROWS, ROWS)
         shared(128)
         from_x(9)
@@ -729,12 +744,6 @@
         weight_ready(4)
         weight_ready(5)
 
-    grads_ready(2, 1)
-    out_ref[0] += back(2, 1)
-    grads_ready(3, 1)
-    grad_norm = out_ref[0] + back(3, 1)
-    out_ref[0] = norm_backward(grad_norm, normed_buf[...], inverse_buf[...], gain_ref[...][None])
-
     for c in range(len(CHUNKS)):
         x_copy(c, w).wait_send()
         y_copy(c, g).wait_send()
@@ -770,6 +779,11 @@
                 send_grads(h, 0).wait_send()
 
     grads_sent((0, 1))
+    grads_ready(2, 1)
+    out_ref[0] += back(2, 1)
+    grads_ready(3, 1)
+    grad_norm = out_ref[0] + back(3, 1)
+    out_ref[0] = norm_backward(grad_norm, normed_buf[...], inverse_buf[...], gain_ref[...][None])
 
     @pl.when(inner)
     def _():
@@ -816,6 +830,7 @@
             pltpu.VMEM((ROWS, WIDTH), BF16),
             pltpu.VMEM((HD, ROWS), BF16),
             pltpu.VMEM((4, 2 * BLOCK, ROWS), BF16),
+            pltpu.VMEM((4 * ROWS, 3 * BLOCK), F32),
             pltpu.VMEM((2, 3, BLOCK, 4 * ROWS), BF16),
             pltpu.VMEM((4, 4, 3, HEAD_DIM, ROWS), BF16),
             pltpu.VMEM((3, HD, ROWS), BF16),

time: 41.5 us -> 40.6 us (0.978)
  Pallas kernels: 39.2 us -> 38.3 us
    pallas_call x1, Pallas kernels: 39.2 us -> 38.3 us  [fused(): pl.pallas_call(fused_kernel, out_shape=jax.ShapeDtypeStruct((1, ROWS, WID...]
where the time goes in v5:
time: 40.6 us; the launch traced here: 40.4 us
  Pallas kernels  38.3 us (94%)
  local copies, waits for them, and re-layouts  2.07 us (5%)
    pallas_call x1, Pallas kernels, fused(): pl.pallas_call(fused_kernel, out_shape=jax.ShapeDtypeStruct((1, ROWS, WID...  38.3 us
    unnamed x1, local copies, waits for them, and re-layouts  2.07 us

profile of v5, /device:TPU:1, one launch (start us, length us, event | category | flops | bytes accessed | tf_op | source)
XLA Modules:
  0.0 40.4 jit_solution(13243481546880359571)
XLA Ops:
  0.0 38.3 %shard_map.100 = f32[1,128,1536]{2,1,0:T(8,128)} custom-call(bf16[1,128,1536]{2,1,0:T(8,128)(2,1)} %tokens_hbm.1, bf16[1,128,1536]{2,1,0:T(8,128)(2,1)} %upstream_hbm.1, f32[1536]{0:T(1024)} %gain_hbm.1, f32[1536]{0:T(1024)} %norm_bias_hbm.1, bf16[384,2304]{1,0:T(8,128)(2,1)} %codes_hbm.1, f32[3,18]{1,0:T(4,128)} %in_scales_hbm.1, f32[2304]{0:T(1024)} %in_bias_hbm.1, ...), custom_call_target="tpu_custom_call" | custom-call | flops 2500000000 | bytes 8000000 | tf_op jit(solution)/shard_map/pallas_call | solution.py:807
  38.3 2.1 %copy.12 = f32[1,128,1536]{2,1,0:T(8,128)} copy(f32[1,128,1536]{2,1,0:T(8,128)} %shard_map.100) | data formatting | bytes 1572864

commit v6 on v5

--- a/solution.py
+++ b/solution.py
@@ -488,7 +488,9 @@
         for part in range(PARTS):
             send_tokens(part).start()
 
-    share_all()
+    @pl.when(outer | home)
+    def _():
+        share_all()
 
     load_gain.wait()
     load_norm_bias.wait()
@@ -529,6 +531,11 @@
     relay_inner(2, 2)
     relay_inner(1, 0, 1)
     from_x(1)
+
+    @pl.when(inner & away)
+    def _():
+        share_all()
+
     relay_outer(1, 2, 3)
     from_x(2)
     relay_inner(2, 3)
@@ -614,13 +621,14 @@
 
     @pl.when(inner)
     def _():
-        await_tokens(2, 3)
+        await_tokens(2)
         normalize_slot(2)
+        from_x(5)
+        from_y(3)
+        await_tokens(3)
         normalize_slot(3)
-        from_x(5)
         weight_near(core)
         project_near(0, 0, 4 * ROWS)
-        from_y(3)
         from_x(6)
         weight_ready(core, False)
         project(0, 0, 4 * ROWS)
@@ -718,10 +726,12 @@
         weight_ready(2)
         weight_ready(3)
 
+    grads_ready(0, 1)
+    out_ref[0] = back(0, 1)
     from_y(10)
     from_y(11)
-    grads_ready(0, 2)
-    out_ref[0] = back(0, 2)
+    grads_ready(1, 1)
+    out_ref[0] += back(1, 1)
 
     @pl.when(inner)
     def _():

time: 40.6 us -> 40.2 us (level)
  the two profiles are of different devices: /device:TPU:1 before, /device:TPU:0 now
where the time goes in v6:
time: 40.2 us; the launch traced here: 40 us
  Pallas kernels  38 us (95%)
  local copies, waits for them, and re-layouts  2.07 us (5%)
    pallas_call x1, Pallas kernels, fused(): pl.pallas_call(fused_kernel, out_shape=jax.ShapeDtypeStruct((1, ROWS, WID...  38 us
    unnamed x1, local copies, waits for them, and re-layouts  2.07 us

profile of v6, /device:TPU:0, one launch (start us, length us, event | category | flops | bytes accessed | tf_op | source)
XLA Modules:
  0.0 40.0 jit_solution(5856009995380293892)
XLA Ops:
  0.0 38.0 %shard_map.100 = f32[1,128,1536]{2,1,0:T(8,128)} custom-call(bf16[1,128,1536]{2,1,0:T(8,128)(2,1)} %tokens_hbm.1, bf16[1,128,1536]{2,1,0:T(8,128)(2,1)} %upstream_hbm.1, f32[1536]{0:T(1024)} %gain_hbm.1, f32[1536]{0:T(1024)} %norm_bias_hbm.1, bf16[384,2304]{1,0:T(8,128)(2,1)} %codes_hbm.1, f32[3,18]{1,0:T(4,128)} %in_scales_hbm.1, f32[2304]{0:T(1024)} %in_bias_hbm.1, ...), custom_call_target="tpu_custom_call" | custom-call | flops 2500000000 | bytes 8000000 | tf_op jit(solution)/shard_map/pallas_call | solution.py:817
  38.0 2.1 %copy.12 = f32[1,128,1536]{2,1,0:T(8,128)} copy(f32[1,128,1536]{2,1,0:T(8,128)} %shard_map.100) | data formatting | bytes 1572864

commit v7 on v6

--- a/solution.py
+++ b/solution.py
@@ -583,6 +583,11 @@
         b = block_at(h // 2 * 2 + core)
         return grad_copy(h, slot, b, {"seq": blocks[slot], "weight": owner})
 
+    def send_across(h, turn):
+        b = block_at(h // 2 * 2 + core)
+        slot = 2 + side if turn == 0 else 3 - side
+        return grad_copy(h, slot, b, {"seq": turn + 2 - 2 * side, "weight": owner})
+
     def attend(h):
         n, i = h // 2, h % 2
         rows = slice(HEAD_DIM * i, HEAD_DIM * (i + 1))
@@ -604,10 +609,12 @@
             value = parts[t].astype(BF16)
             for slot in range(4):
                 grads[h, slot, t] = value[:, ROWS * slot : ROWS * (slot + 1)]
-        for slot in (3, 1) if h == 2 else (3, 2, 1):
-            send_grads(h, slot).start()
-        if h == 3:
-            send_grads(2, 2).start()
+        send_across(h, 0).start()
+        if h % 2 == 1:
+            send_across(h, 1).start()
+        send_grads(h, 1).start()
+        if h % 2 == 1:
+            send_across(h - 1, 1).start()
 
         @pl.when(home)
         def _():

time: 40.2 us -> 40 us (level)
  the two profiles are of different devices: /device:TPU:0 before, /device:TPU:1 now
where the time goes in v7:
time: 40 us; the launch traced here: 39.5 us
  Pallas kernels  37.5 us (94%)
  local copies, waits for them, and re-layouts  2.07 us (5%)
    pallas_call x1, Pallas kernels, fused(): pl.pallas_call(fused_kernel, out_shape=jax.ShapeDtypeStruct((1, ROWS, WID...  37.5 us
    unnamed x1, local copies, waits for them, and re-layouts  2.07 us

profile of v7, /device:TPU:1, one launch (start us, length us, event | category | flops | bytes accessed | tf_op | source)
XLA Modules:
  0.0 39.5 jit_solution(16758001280789265977)
XLA Ops:
  0.0 37.5 %shard_map.100 = f32[1,128,1536]{2,1,0:T(8,128)} custom-call(bf16[1,128,1536]{2,1,0:T(8,128)(2,1)} %tokens_hbm.1, bf16[1,128,1536]{2,1,0:T(8,128)(2,1)} %upstream_hbm.1, f32[1536]{0:T(1024)} %gain_hbm.1, f32[1536]{0:T(1024)} %norm_bias_hbm.1, bf16[384,2304]{1,0:T(8,128)(2,1)} %codes_hbm.1, f32[3,18]{1,0:T(4,128)} %in_scales_hbm.1, f32[2304]{0:T(1024)} %in_bias_hbm.1, ...), custom_call_target="tpu_custom_call" | custom-call | flops 2500000000 | bytes 8000000 | tf_op jit(solution)/shard_map/pallas_call | solution.py:824
  37.5 2.1 %copy.12 = f32[1,128,1536]{2,1,0:T(8,128)} copy(f32[1,128,1536]{2,1,0:T(8,128)} %shard_map.100) | data formatting | bytes 1572864

commit v8 on v7

--- a/solution.py
+++ b/solution.py
@@ -214,6 +214,7 @@
     scaled,
     packed,
     gathered,
+    total,
     partial,
     projected,
     grads,
@@ -715,14 +716,14 @@
                     grad_copy(i, 0, b, {"weight": sibling}).wait_recv()
 
     def back(first, count):
-        total = None
+        result = None
         part = slice(BLOCK * first, BLOCK * (first + count))
         for t in range(3):
             term = lax.dot_general(
                 grad_proj[t, part, :].T, weight[t, :, part], NT, preferred_element_type=F32
             )
-            total = term if total is None else total + term
-        return total
+            result = term if result is None else result + term
+        return result
 
     @pl.when(inner)
     def _():
@@ -734,11 +735,11 @@
         weight_ready(3)
 
     grads_ready(0, 1)
-    out_ref[0] = back(0, 1)
+    total[...] = back(0, 1)
     from_y(10)
     from_y(11)
     grads_ready(1, 1)
-    out_ref[0] += back(1, 1)
+    total[...] += back(1, 1)
 
     @pl.when(inner)
     def _():
@@ -750,7 +751,7 @@
         weight_ready(1 - core)
 
     grads_ready(4, 2)
-    out_ref[0] += back(4, 2)
+    total[...] += back(4, 2)
 
     @pl.when(inner)
     def _():
@@ -797,10 +798,11 @@
 
     grads_sent((0, 1))
     grads_ready(2, 1)
-    out_ref[0] += back(2, 1)
+    total[...] += back(2, 1)
     grads_ready(3, 1)
-    grad_norm = out_ref[0] + back(3, 1)
-    out_ref[0] = norm_backward(grad_norm, normed_buf[...], inverse_buf[...], gain_ref[...][None])
+    grad_norm = total[...] + back(3, 1)
+    result = norm_backward(grad_norm, normed_buf[...], inverse_buf[...], gain_ref[...][None])
+    out_ref[0] = result.astype(BF16)
 
     @pl.when(inner)
     def _():
@@ -823,7 +825,7 @@
     vmem = pl.BlockSpec(memory_space=pltpu.VMEM)
     return pl.pallas_call(
         fused_kernel,
-        out_shape=jax.ShapeDtypeStruct((1, ROWS, WIDTH), F32),
+        out_shape=jax.ShapeDtypeStruct((1, ROWS, WIDTH), BF16),
         in_specs=[hbm] * 10,
         out_specs=vmem,
         scratch_shapes=[
@@ -847,6 +849,7 @@
             pltpu.VMEM((ROWS, WIDTH), BF16),
             pltpu.VMEM((HD, ROWS), BF16),
             pltpu.VMEM((4, 2 * BLOCK, ROWS), BF16),
+            pltpu.VMEM((ROWS, WIDTH), F32),
             pltpu.VMEM((4 * ROWS, 3 * BLOCK), F32),
             pltpu.VMEM((2, 3, BLOCK, 4 * ROWS), BF16),
             pltpu.VMEM((4, 4, 3, HEAD_DIM, ROWS), BF16),
@@ -879,7 +882,7 @@
         output_codes,
         output_scales,
         layer_scale,
-    )
+    ).astype(F32)
 
 
 def solution(mesh):

time: 40 us -> 39.8 us (level)
  local copies, waits for them, and re-layouts: 2.07 us -> 0 us
  other arithmetic: 0 us -> 1.95 us
    unnamed x1 -> x0, local copies, waits for them, and re-layouts: 2.07 us -> none
    convert_element_type x0 -> x1, other arithmetic: none -> 1.95 us  [fused(): return pl.pallas_call(fused_kernel, out_shape=jax.ShapeDtypeStruct((1, RO...]
where the time goes in v8:
time: 39.8 us; the launch traced here: 39.3 us
  Pallas kernels  37.4 us (94%)
  other arithmetic  1.95 us (5%)
    pallas_call x1, Pallas kernels, fused(): pl.pallas_call(fused_kernel, out_shape=jax.ShapeDtypeStruct((1, ROWS, WID...  37.4 us
    convert_element_type x1, other arithmetic, fused(): return pl.pallas_call(fused_kernel, out_shape=jax.ShapeDtypeStruct((1, RO...  1.95 us

profile of v8, /device:TPU:1, one launch (start us, length us, event | category | flops | bytes accessed | tf_op | source)
XLA Modules:
  0.0 39.3 jit_solution(13282732032978341960)
XLA Ops:
  0.0 37.4 %shard_map.100 = bf16[1,128,1536]{2,1,0:T(8,128)(2,1)} custom-call(bf16[1,128,1536]{2,1,0:T(8,128)(2,1)} %tokens_hbm.1, bf16[1,128,1536]{2,1,0:T(8,128)(2,1)} %upstream_hbm.1, f32[1536]{0:T(1024)} %gain_hbm.1, f32[1536]{0:T(1024)} %norm_bias_hbm.1, bf16[384,2304]{1,0:T(8,128)(2,1)} %codes_hbm.1, f32[3,18]{1,0:T(4,128)} %in_scales_hbm.1, f32[2304]{0:T(1024)} %in_bias_hbm.1, ...), custom_call_target="tpu_custom_call" | custom-call | flops 2500000000 | bytes 8000000 | tf_op jit(solution)/shard_map/pallas_call | solution.py:826
  37.4 2.0 %convert_element_type.3 = f32[1,128,1536]{2,1,0:T(8,128)} convert(bf16[1,128,1536]{2,1,0:T(8,128)(2,1)} %shard_map.100) | non-fusion elementwise | flops 196608 | bytes 1179648 | tf_op jit(solution)/shard_map/convert_element_type | solution.py:885
